TPU v7x, 256 devices: a whole 4x4x8 slice. The times are simulated.
256 devices in a mesh: ctx: 32 (over z_hi, y, x), tp: 8 (over z_lo, core).
Axes of the slice: x: 4, y: 4, z: 8 (z_hi: 2, z_lo: 4; z = z_hi * 4 + z_lo), core: 2. Of those that a mesh axis runs over, the one named last changes fastest.
Arguments:
- features: bfloat16 [3, 8192, 4096], P(None, 'tp', 'ctx'), may hold values from -6 to 6
- short_filters: bfloat16 [3, 3, 8192], P(None, None, 'tp'), may hold values from -3 to 3
- long_filter: bfloat16 [8192, 4096], P('tp', 'ctx'), may hold values from -0.09375 to 0.09375
- cotangent: bfloat16 [8192, 4096], P('tp', 'ctx'), may hold values from -6 to 6
Outputs:
- feature_grads: float32 [3, 8192, 4096], P(None, 'tp', 'ctx')
- short_grads: float32 [3, 3, 8192], P(None, None, 'tp')
- long_grads: float32 [8192, 4096], P('tp', 'ctx')
All inputs are finite; a program needn't handle non-finite values.
Results may differ from a plain program's by a relative error of at most 0.0041.
Values may be sent and summed in bfloat16 or wider, within the bound.
A program may use at most 64 MiB of HBM per device.

v0:
```python
import math

import jax
import jax.numpy as jnp
from jax import lax
from jax.sharding import PartitionSpec as P


def from_behind(array, axis, by):
    size = lax.axis_size(axis)
    pairs = [(i, i + by) for i in range(size) if 0 <= i + by < size]
    return lax.ppermute(array, axis, pairs)


def spectral_einsum(form, left, right):
    return jnp.einsum(form, left, right, precision=lax.Precision.HIGH)


def rotation(rows, cols, modulus, sign):
    product = (
        lax.broadcasted_iota(jnp.int32, (rows, cols), 0)
        * lax.broadcasted_iota(jnp.int32, (rows, cols), 1)
        % modulus
    )
    angle = sign * 2.0 * math.pi / modulus * product.astype(jnp.float32)
    return (jnp.cos(angle), jnp.sin(angle))


def spectral_tables(total):
    inner = 128
    outer = total // inner
    return (
        rotation(outer, outer, outer, -1.0),
        rotation(outer, inner, total, -1.0),
        rotation(inner, inner, inner, -1.0),
    )


def forward_spectrum(signal, tables, total):
    first, twiddle, second = tables
    channels, length = signal.shape
    outer = first[0].shape[0]
    padded = jnp.pad(signal, ((0, 0), (0, total - length))).reshape(channels, outer, total // outer)
    real_part = spectral_einsum("kn,cnm->ckm", first[0], padded)
    imag_part = spectral_einsum("kn,cnm->ckm", first[1], padded)
    turned_real = real_part * twiddle[0] - imag_part * twiddle[1]
    turned_imag = real_part * twiddle[1] + imag_part * twiddle[0]
    spec_real = spectral_einsum("ckm,mj->ckj", turned_real, second[0]) - spectral_einsum(
        "ckm,mj->ckj", turned_imag, second[1]
    )
    spec_imag = spectral_einsum("ckm,mj->ckj", turned_real, second[1]) + spectral_einsum(
        "ckm,mj->ckj", turned_imag, second[0]
    )
    return (spec_real, spec_imag)


def inverse_signal(spec_real, spec_imag, tables, total, length):
    first, twiddle, second = tables
    channels = spec_real.shape[0]
    part_real = spectral_einsum("ckj,mj->ckm", spec_real, second[0]) + spectral_einsum(
        "ckj,mj->ckm", spec_imag, second[1]
    )
    part_imag = spectral_einsum("ckj,mj->ckm", spec_imag, second[0]) - spectral_einsum(
        "ckj,mj->ckm", spec_real, second[1]
    )
    turned_real = part_real * twiddle[0] + part_imag * twiddle[1]
    turned_imag = part_imag * twiddle[0] - part_real * twiddle[1]
    signal = spectral_einsum("nk,ckm->cnm", first[0], turned_real) + spectral_einsum(
        "nk,ckm->cnm", first[1], turned_imag
    )
    return signal.reshape(channels, total)[:, :length] / total


def long_core(gated, outer, filt):
    length = gated.shape[1]
    total = 2 * length
    tables = spectral_tables(total)
    filt_real, filt_imag = forward_spectrum(filt, tables, total)
    gate_real, gate_imag = forward_spectrum(gated, tables, total)
    outer_real, outer_imag = forward_spectrum(outer, tables, total)
    conv_out = inverse_signal(
        filt_real * gate_real - filt_imag * gate_imag,
        filt_real * gate_imag + filt_imag * gate_real,
        tables,
        total,
        length,
    )
    gate_grad = inverse_signal(
        filt_real * outer_real + filt_imag * outer_imag,
        filt_real * outer_imag - filt_imag * outer_real,
        tables,
        total,
        length,
    )
    filt_grad = inverse_signal(
        outer_real * gate_real + outer_imag * gate_imag,
        outer_imag * gate_real - outer_real * gate_imag,
        tables,
        total,
        length,
    )
    return (conv_out, gate_grad, filt_grad)


def short_conv(padded, weights, length):
    width = weights.shape[1]
    total = jnp.zeros(padded.shape[:-1] + (length,), jnp.float32)
    for offset in range(width):
        start = width - 1 - offset
        total = total + weights[:, offset, :, None] * padded[..., start : start + length]
    return total


def body(features, short_filters, long_filter, cotangent):
    length_dev = features.shape[-1]
    width = short_filters.shape[1]
    rim = from_behind(features[..., length_dev - (width - 1) :], "ctx", 1)
    signal = features.astype(jnp.float32)
    weights = short_filters.astype(jnp.float32)
    padded = jnp.concatenate([rim.astype(jnp.float32), signal], axis=-1)
    mixed = short_conv(padded, weights, length_dev)
    upstream = cotangent.astype(jnp.float32)
    gated = (mixed[1] * mixed[2]).astype(jnp.bfloat16)
    outer = (upstream * mixed[0]).astype(jnp.bfloat16)
    moved = (
        lax.all_to_all(gated, "ctx", split_axis=0, concat_axis=1, tiled=True),
        lax.all_to_all(outer, "ctx", split_axis=0, concat_axis=1, tiled=True),
        lax.all_to_all(long_filter, "ctx", split_axis=0, concat_axis=1, tiled=True),
    )
    conv_full, grad_full, filt_full = long_core(
        moved[0].astype(jnp.float32), moved[1].astype(jnp.float32), moved[2].astype(jnp.float32)
    )
    back = (
        lax.all_to_all(conv_full, "ctx", split_axis=1, concat_axis=0, tiled=True),
        lax.all_to_all(grad_full, "ctx", split_axis=1, concat_axis=0, tiled=True),
        lax.all_to_all(filt_full, "ctx", split_axis=1, concat_axis=0, tiled=True),
    )
    conv_out, gate_grad, filt_grad = back
    branch_grads = jnp.stack([upstream * conv_out, gate_grad * mixed[2], gate_grad * mixed[1]])
    next_rim = from_behind(branch_grads[..., : width - 1], "ctx", -1)
    trailing = jnp.concatenate([branch_grads, next_rim], axis=-1)
    feature_grads = jnp.zeros(branch_grads.shape, jnp.float32)
    for offset in range(width):
        feature_grads = (
            feature_grads
            + weights[:, offset, :, None] * trailing[..., offset : offset + length_dev]
        )
    local_short = jnp.stack(
        [
            jnp.sum(
                branch_grads * padded[..., width - 1 - offset : width - 1 - offset + length_dev],
                axis=-1,
            )
            for offset in range(width)
        ],
        axis=1,
    )
    short_grads = lax.psum(local_short, "ctx")
    return (feature_grads, short_grads, filt_grad)


def solution(mesh):
    return jax.shard_map(
        body,
        mesh=mesh,
        in_specs=(P(None, "tp", "ctx"), P(None, None, "tp"), P("tp", "ctx"), P("tp", "ctx")),
        out_specs=(P(None, "tp", "ctx"), P(None, None, "tp"), P("tp", "ctx")),
        check_vma=False,
    )
```

profile of v0, /device:TPU:160, one launch (start us, length us, event | category | flops | bytes accessed | tf_op | source)
XLA Modules:
  0.0 386.7 jit_solution(7861689573957313367)
XLA Ops:
  0.7 1.5 slice.54
  2.5 3.4 collective-permute-start
  5.9 12.2 %all-to-all-start = ((bf16[32,32,128]{2,1,0:T(8,128)(2,1)}), bf16[32,32,128]{2,1,0:T(8,128)(2,1)}, u32[]{:S(2)}, u32[]{:S(2)}) async-start(bf16[32,32,128]{2,1,0:T(8,128)(2,1)} %bitcast), calls=%async_computation | async-start | bytes 524288 | tf_op jit(solution)/shard_map/all_to_all | solution.py:128
  18.9 4.3 %multiply_add_fusion = f32[3,1024,128]{2,1,0:T(8,128)S(1)} fusion(f32[3,1024]{1,0:T(4,128)S(1)} %get-tuple-element.37, f32[3,1024]{1,0:T(4,128)S(1)} %get-tuple-element.38, bf16[3,1024,128]{2,1,0:T(8,128)(2,1)} %param.4, f32[3,1024]{1,0:T(4,128)S(1)} %bitcast.210, f32[3,1024,128]{2,1,0:T(8,128)S(1)} %convert_element_type.184, f32[3,1024,2]{2,1,0:T(8,128)S(1)} %copy.52), kind=kLoop, calls=%fused_computation.13 | loop fusion | flops 3145728 | bytes 3993600 | tf_op jit(solution)/shard_map/add | solution.py:110
  23.2 0.9 multiply_convert_fusion
  24.5 0.8 fusion.25
  25.2 3.3 all-to-all-done
  28.6 9.0 %all-to-all-start.1 = ((bf16[32,32,128]{2,1,0:T(8,128)(2,1)}), bf16[32,32,128]{2,1,0:T(8,128)(2,1)S(1)}, u32[]{:S(2)}, u32[]{:S(2)}) async-start(bf16[32,32,128]{2,1,0:T(8,128)(2,1)} %bitcast.8), calls=%async_computation.1 | async-start | bytes 524288 | tf_op jit(solution)/shard_map/all_to_all | solution.py:126
  37.6 1.0 copy_bitcast_fusion.8
  39.9 0.8 fusion.41
  40.7 1.8 convolution_add_fusion.8
  42.5 0.8 fusion.42
  43.4 1.8 convolution_subtract_fusion.5
  45.2 2.1 all-to-all-done.1
  47.3 10.4 %all-to-all-start.3 = ((bf16[32,32,128]{2,1,0:T(8,128)(2,1)}), bf16[32,32,128]{2,1,0:T(8,128)(2,1)}, u32[]{:S(2)}, u32[]{:S(2)}) async-start(bf16[32,32,128]{2,1,0:T(8,128)(2,1)} %bitcast.17), calls=%async_computation.3 | async-start | bytes 524288 | tf_op jit(solution)/shard_map/all_to_all | solution.py:127
  59.0 7.7 %all-to-all-done.3 = bf16[32,32,128]{2,1,0:T(8,128)(2,1)} async-done(((bf16[32,32,128]{2,1,0:T(8,128)(2,1)}), bf16[32,32,128]{2,1,0:T(8,128)(2,1)}, u32[]{:S(2)}, u32[]{:S(2)}) %all-to-all-start.3) | async-done | bytes 262176 | tf_op jit(solution)/shard_map/all_to_all | solution.py:127
  66.7 1.0 copy_bitcast_fusion.6
  68.9 0.8 fusion.44
  69.8 0.8 fusion.43
  70.6 0.8 fusion.46
  71.5 0.8 fusion.45
  72.3 0.8 convolution_subtract_fusion.4
  73.2 0.8 convolution_subtract_fusion.2
  74.1 0.8 convolution_add_fusion.7
  75.6 2.3 multiply_add_fusion.1
  77.9 0.8 fusion.74
  78.7 0.8 fusion.72
  79.6 1.0 convolution_add_fusion.6
  80.6 0.8 convolution_subtract_fusion.3
  81.5 0.7 fusion.20
  82.2 0.7 convolution_add_fusion.5
  83.0 0.6 copy.91
  83.6 0.8 copy_bitcast_fusion.5
  84.4 9.7 %all-to-all-start.2 = ((f32[32,32,128]{2,0,1:T(8,128)}), f32[32,32,128]{2,0,1:T(8,128)}, u32[]{:S(2)}, u32[]{:S(2)}) async-start(f32[32,32,128]{2,0,1:T(8,128)} %copy_bitcast_fusion.5), calls=%async_computation.2 | async-start | bytes 1048576 | tf_op jit(solution)/shard_map/all_to_all | solution.py:134
  94.1 0.8 fusion.68
  95.4 0.8 fusion.66
  96.2 0.8 convolution_add_fusion.3
  97.0 0.8 convolution_subtract_fusion.1
  97.9 0.7 fusion.13
  98.6 0.8 convolution_add_fusion.2
  100.0 0.9 copy_bitcast_fusion.4
  100.8 0.8 fusion.64
  101.7 1.8 fusion.62
  103.5 0.8 convolution_add_fusion.1
  104.3 2.5 all-to-all-done.2
  106.8 10.3 %all-to-all-start.4 = ((f32[32,32,128]{2,0,1:T(8,128)}), f32[32,32,128]{2,0,1:T(8,128)}, u32[]{:S(2)}, u32[]{:S(2)}) async-start(f32[32,32,128]{2,0,1:T(8,128)} %copy_bitcast_fusion.4), calls=%async_computation.4 | async-start | bytes 1048576 | tf_op jit(solution)/shard_map/all_to_all | solution.py:135
  117.1 2.0 convolution_subtract_fusion
  119.1 0.7 fusion.6
  119.9 0.8 convolution_add_fusion
  120.6 0.6 copy.89
  121.3 0.9 copy_bitcast_fusion.3
  122.1 7.3 %all-to-all-done.4 = f32[32,32,128]{2,0,1:T(8,128)} async-done(((f32[32,32,128]{2,0,1:T(8,128)}), f32[32,32,128]{2,0,1:T(8,128)}, u32[]{:S(2)}, u32[]{:S(2)}) %all-to-all-start.4) | async-done | bytes 524320 | tf_op jit(solution)/shard_map/all_to_all | solution.py:135
  129.4 9.6 %all-to-all-start.5 = ((f32[32,32,128]{2,0,1:T(8,128)}), f32[32,32,128]{2,0,1:T(8,128)}, u32[]{:S(2)}, u32[]{:S(2)}) async-start(f32[32,32,128]{2,0,1:T(8,128)} %copy_bitcast_fusion.3), calls=%async_computation.5 | async-start | bytes 1048576 | tf_op jit(solution)/shard_map/all_to_all | solution.py:136
  139.1 1.1 fusion.24
  140.2 1.1 bitcast_multiply_fusion.1
  141.4 0.6 copy.57
  142.0 6.7 %collective-permute-start.1 = (f32[3,1024,2]{1,0,2:T(4,128)S(1)}, f32[3,1024,2]{1,0,2:T(4,128)S(1)}, u32[]{:S(2)}, u32[]{:S(2)}) collective-permute-start(f32[3,1024,2]{1,0,2:T(4,128)S(1)} %copy.57), channel_id=1, source_target_pairs={{8,0},{16,8},{24,16},{32,24},{40,32},{48,40},{56,48},{64,56},{72,6... | collective-permute-start | bytes 73736 | tf_op jit(solution)/shard_map/ppermute | solution.py:12
  148.7 0.6 all-to-all-done.5
  149.4 0.9 collective-permute-done.1
  151.1 1.1 copy-done.1
  152.9 5.8 %multiply_reduce_fusion.1 = (f32[3,1024]{1,0:T(4,128)S(1)}, f32[3,1024]{1,0:T(4,128)S(1)}, f32[3,1024]{1,0:T(4,128)S(1)}, f32[3,1024,128]{2,1,0:T(8,128)}) fusion(f32[3,1024,128]{2,1,0:T(8,128)S(1)} %copy-done.1, f32[3,1024,2]{2,1,0:T(8,128)S(1)} %copy-done.3, f32[1,1024,128]{2,1,0:T(8,128)S(1)} %get-tuple-element.32, ...), kind=kLoop, calls=%fused_computation.11 | loop fusion | flops 6282240 | bytes 8749056 | tf_op jit(solution)/shard_map/reduce_sum | solution.py:150
  158.7 225.1 %psum.7 = f32[3,3,1024]{2,0,1:T(4,128)S(1)} all-reduce(f32[3,3,1024]{2,0,1:T(4,128)S(1)} %pad_maximum_fusion.3), channel_id=1, replica_groups=mesh['ctx'=32,'tp'=8] {'ctx'}, use_global_device_ids=true, to_apply=%region_3.4 | all-reduce | flops 9216 | bytes 73728 | tf_op jit(solution)/shard_map/psum | solution.py:158
  383.8 0.6 copy.60
  384.4 1.9 copy.94
  (51 shorter events, 8.3 us)
Async XLA Ops:
  0.6 17.8 %copy-start.4 = (bf16[3,1024,128]{2,1,0:T(8,128)(2,1)S(1)}, bf16[3,1024,128]{2,1,0:T(8,128)(2,1)}, u32[]{:S(2)}) copy-start(bf16[3,1024,128]{2,1,0:T(8,128)(2,1)} %param.4) | copy-start | bytes 2359300
  0.6 17.5 %copy-start.12 = (bf16[3,3,1024]{2,1,0:T(4,128)(2,1)S(1)}, bf16[3,3,1024]{2,1,0:T(4,128)(2,1)}, u32[]{:S(2)}) copy-start(bf16[3,3,1024]{2,1,0:T(4,128)(2,1)} %param.5) | copy-start | bytes 55300
  2.5 16.0 %collective-permute-start = (bf16[3,1024,2]{1,0,2:T(4,128)(2,1)S(1)}, bf16[3,1024,2]{1,0,2:T(4,128)(2,1)S(1)}, u32[]{:S(2)}, u32[]{:S(2)}) collective-permute-start(bf16[3,1024,2]{1,0,2:T(4,128)(2,1)S(1)} %copy.64), channel_id=1, source_target_pairs={{0,8},{8,16},{16,24},{24,32},{32,40},{40,48},{48,56},{56,64},{64,7... | collective-permute-start | bytes 36872 | tf_op jit(solution)/shard_map/ppermute | solution.py:12
  5.9 22.6 %all-to-all-start = ((bf16[32,32,128]{2,1,0:T(8,128)(2,1)}), bf16[32,32,128]{2,1,0:T(8,128)(2,1)}, u32[]{:S(2)}, u32[]{:S(2)}) async-start(bf16[32,32,128]{2,1,0:T(8,128)(2,1)} %bitcast), calls=%async_computation | async-start | bytes 524288 | tf_op jit(solution)/shard_map/all_to_all | solution.py:128
  18.5 4.7 %copy-start = (f32[3,1024,128]{2,1,0:T(8,128)}, f32[3,1024,128]{2,1,0:T(8,128)S(1)}, u32[]{:S(2)}) copy-start(f32[3,1024,128]{2,1,0:T(8,128)S(1)} %convert_element_type.184) | copy-start | bytes 4718596
  18.9 4.3 %copy-start.2 = (f32[3,1024,2]{2,1,0:T(8,128)}, f32[3,1024,2]{2,1,0:T(8,128)S(1)}, u32[]{:S(2)}) copy-start(f32[3,1024,2]{2,1,0:T(8,128)S(1)} %copy.52) | copy-start | bytes 73732
  18.9 5.6 %copy-start.11 = (bf16[1024,128]{1,0:T(8,128)(2,1)S(1)}, bf16[1024,128]{1,0:T(8,128)(2,1)}, u32[]{:S(2)}) copy-start(bf16[1024,128]{1,0:T(8,128)(2,1)} %param.7) | copy-start | bytes 786436
  23.2 1.2 copy-start.6
  28.6 18.7 %all-to-all-start.1 = ((bf16[32,32,128]{2,1,0:T(8,128)(2,1)}), bf16[32,32,128]{2,1,0:T(8,128)(2,1)S(1)}, u32[]{:S(2)}, u32[]{:S(2)}) async-start(bf16[32,32,128]{2,1,0:T(8,128)(2,1)} %bitcast.8), calls=%async_computation.1 | async-start | bytes 524288 | tf_op jit(solution)/shard_map/all_to_all | solution.py:126
  47.3 19.4 %all-to-all-start.3 = ((bf16[32,32,128]{2,1,0:T(8,128)(2,1)}), bf16[32,32,128]{2,1,0:T(8,128)(2,1)}, u32[]{:S(2)}, u32[]{:S(2)}) async-start(bf16[32,32,128]{2,1,0:T(8,128)(2,1)} %bitcast.17), calls=%async_computation.3 | async-start | bytes 524288 | tf_op jit(solution)/shard_map/all_to_all | solution.py:127
  74.1 1.2 copy-start.9
  74.1 1.5 copy-start.10
  84.4 22.3 %all-to-all-start.2 = ((f32[32,32,128]{2,0,1:T(8,128)}), f32[32,32,128]{2,0,1:T(8,128)}, u32[]{:S(2)}, u32[]{:S(2)}) async-start(f32[32,32,128]{2,0,1:T(8,128)} %copy_bitcast_fusion.5), calls=%async_computation.2 | async-start | bytes 1048576 | tf_op jit(solution)/shard_map/all_to_all | solution.py:134
  94.1 1.2 copy-start.8
  106.8 22.6 %all-to-all-start.4 = ((f32[32,32,128]{2,0,1:T(8,128)}), f32[32,32,128]{2,0,1:T(8,128)}, u32[]{:S(2)}, u32[]{:S(2)}) async-start(f32[32,32,128]{2,0,1:T(8,128)} %copy_bitcast_fusion.4), calls=%async_computation.4 | async-start | bytes 1048576 | tf_op jit(solution)/shard_map/all_to_all | solution.py:135
  121.3 18.9 %copy-start.7 = (f32[3,1024,128]{2,1,0:T(8,128)S(1)}, f32[3,1024,128]{2,1,0:T(8,128)}, u32[]{:S(2)}) copy-start(f32[3,1024,128]{2,1,0:T(8,128)} %copy-done.6) | copy-start | bytes 4718596
  129.4 19.9 %all-to-all-start.5 = ((f32[32,32,128]{2,0,1:T(8,128)}), f32[32,32,128]{2,0,1:T(8,128)}, u32[]{:S(2)}, u32[]{:S(2)}) async-start(f32[32,32,128]{2,0,1:T(8,128)} %copy_bitcast_fusion.3), calls=%async_computation.5 | async-start | bytes 1048576 | tf_op jit(solution)/shard_map/all_to_all | solution.py:136
  142.0 8.3 %collective-permute-start.1 = (f32[3,1024,2]{1,0,2:T(4,128)S(1)}, f32[3,1024,2]{1,0,2:T(4,128)S(1)}, u32[]{:S(2)}, u32[]{:S(2)}) collective-permute-start(f32[3,1024,2]{1,0,2:T(4,128)S(1)} %copy.57), channel_id=1, source_target_pairs={{8,0},{16,8},{24,16},{32,24},{40,32},{48,40},{56,48},{64,56},{72,6... | collective-permute-start | bytes 73736 | tf_op jit(solution)/shard_map/ppermute | solution.py:12
  150.8 1.4 copy-start.1
  150.8 1.9 copy-start.3
  150.8 2.1 copy-start.5
where the time goes:
time: 394 us; the launch traced here: 387 us
  blocking collectives  225 us (57%)
  starting transfers between devices  71.3 us (18%)
  matrix products  33.6 us (9%)
  waiting for transfers between devices  24.5 us (6%)
  other arithmetic  17.1 us (4%)
  local copies, waits for them, and re-layouts  13.4 us (3%)
    psum x1, blocking collectives, body(): short_grads = lax.psum(local_short, 'ctx')  225 us
    dot_general x36, matrix products, spectral_einsum(): return jnp.einsum(form, left, right, precision=lax.Precision.HIGH)  33.6 us
    all_to_all x1, starting transfers between devices, body(): lax.all_to_all(long_filter, 'ctx', split_axis=0, concat_axis=1, tiled=True)  12.2 us
    all_to_all x1, starting transfers between devices, body(): lax.all_to_all(outer, 'ctx', split_axis=0, concat_axis=1, tiled=True)  10.4 us
    all_to_all x1, starting transfers between devices, body(): lax.all_to_all(grad_full, 'ctx', split_axis=1, concat_axis=0, tiled=True)  10.3 us
    ppermute x2, starting transfers between devices, from_behind(): return lax.ppermute(array, axis, pairs)  10.1 us
    all_to_all x1, starting transfers between devices, body(): lax.all_to_all(conv_full, 'ctx', split_axis=1, concat_axis=0, tiled=True)  9.68 us
    all_to_all x1, starting transfers between devices, body(): lax.all_to_all(filt_full, 'ctx', split_axis=1, concat_axis=0, tiled=True)  9.63 us
  transfers between devices with their start and end apart: 8, of which 7 were waited for; matrix products, arithmetic and copies ran while one was open for 9% of the time, Pallas kernels for 0%

commit v1 on v0

v1 whole, which is shorter than its diff:
```python
import functools
import math

import jax
import jax.numpy as jnp
import numpy as np
from jax import lax
from jax.experimental import pallas as pl
from jax.experimental.pallas import tpu as pltpu
from jax.sharding import PartitionSpec as P

MESH = pl.DeviceIdType.MESH
F32, BF16 = jnp.float32, jnp.bfloat16
BLOCKS = 32
PLANE = 16
POS = 128
CH = 1024
OWN = CH // BLOCKS
HALF = OWN // 2
TOTAL = BLOCKS * POS
ROWS = BLOCKS * HALF


def tables():
    k = np.arange(BLOCKS)[:, None] + 0.25
    angle = 2.0 * np.pi * k * np.arange(POS)[None, :] / TOTAL
    turn = np.stack([np.cos(angle), np.sin(angle)], axis=1).astype(np.float32)
    turn = np.broadcast_to(turn[:, :, None, :], (BLOCKS, 2, 8, POS))
    angle = 2.0 * np.pi * np.arange(POS)[:, None] * np.arange(POS)[None, :] / POS
    cos, sin = np.cos(angle), np.sin(angle)
    ahead = np.block([[cos, sin], [-sin, cos]])
    back = np.block([[cos, -sin], [sin, cos]]) / TOTAL

    def split(matrix):
        high = matrix.astype(BF16)
        low = (matrix - high.astype(np.float64)).astype(BF16)
        return np.stack([high, low])

    return np.ascontiguousarray(turn), np.concatenate([split(ahead), split(back)])


def add(a, b):
    return a[0] + b[0], a[1] + b[1]


def sub(a, b):
    return a[0] - b[0], a[1] - b[1]


def quarter(a, sign):
    return (-a[1], a[0]) if sign > 0 else (a[1], -a[0])


def rotate(a, angle):
    c, s = math.cos(angle), math.sin(angle)
    return a[0] * c - a[1] * s, a[0] * s + a[1] * c


def dft4(a, b, c, d, sign):
    e0, e1, o0, o1 = add(a, c), sub(a, c), add(b, d), quarter(sub(b, d), sign)
    return add(e0, o0), add(e1, o1), sub(e0, o0), sub(e1, o1)


def dft8(v, sign):
    even = dft4(v[0], v[2], v[4], v[6], sign)
    odd = dft4(v[1], v[3], v[5], v[7], sign)
    r = math.sqrt(0.5)
    a, b = odd[1], odd[3]
    if sign > 0:
        t1 = ((a[0] - a[1]) * r, (a[0] + a[1]) * r)
        t3 = ((b[0] + b[1]) * -r, (b[0] - b[1]) * r)
    else:
        t1 = ((a[0] + a[1]) * r, (a[1] - a[0]) * r)
        t3 = ((b[1] - b[0]) * r, (b[0] + b[1]) * -r)
    turned = (odd[0], t1, quarter(odd[2], sign), t3)
    return [add(e, t) for e, t in zip(even, turned)] + [sub(e, t) for e, t in zip(even, turned)]


def blocks_ahead(load, stage, turn_ref, store):
    c, s, r = math.cos(math.pi / 8), math.sin(math.pi / 8), math.sqrt(0.5)
    for b0 in range(8):
        x0, x1, x2, x3 = (load(b0 + 8 * b1) for b1 in range(4))
        x2 = x2 * r
        e0, e1 = (x0 + x2, x2), (x0 - x2, -x2)
        u1, u3 = (x1 * c, x1 * s), (x3 * s, x3 * c)
        o0, o1 = add(u1, u3), quarter(sub(u1, u3), 1)
        for k1, value in enumerate((add(e0, o0), add(e1, o1), sub(e0, o0), sub(e1, o1))):
            if b0:
                value = rotate(value, 2.0 * math.pi * (k1 + 0.25) * b0 / 32)
            stage[k1, b0, 0], stage[k1, b0, 1] = value
    for k1 in range(4):
        spectrum = dft8([(stage[k1, b0, 0], stage[k1, b0, 1]) for b0 in range(8)], 1)
        for k0, (re, im) in enumerate(spectrum):
            k = k1 + 4 * k0
            cos, sin = turn_ref[k, 0], turn_ref[k, 1]
            store(k, re * cos - im * sin, re * sin + im * cos)


def blocks_back(load, stage, turn_ref, store):
    for k1 in range(4):
        terms = []
        for k0 in range(8):
            k = k1 + 4 * k0
            re, im = load(k)
            cos, sin = turn_ref[k, 0], turn_ref[k, 1]
            terms.append((re * cos + im * sin, im * cos - re * sin))
        for b0, value in enumerate(dft8(terms, -1)):
            if b0:
                value = rotate(value, -2.0 * math.pi * (k1 + 0.25) * b0 / 32)
            stage[k1, b0, 0], stage[k1, b0, 1] = value
    for b0 in range(8):
        terms = [(stage[k1, b0, 0], stage[k1, b0, 1]) for k1 in range(4)]
        for b1, (re, im) in enumerate(dft4(*terms, -1)):
            angle = math.pi * b1 / 8
            store(b0 + 8 * b1, re * math.cos(angle) + im * math.sin(angle) if b1 else re)


def product(values, weights):
    high = values.astype(BF16)
    low = (values - high.astype(F32)).astype(BF16)
    dot = functools.partial(jnp.dot, preferred_element_type=F32)
    return dot(high, weights[0]) + dot(low, weights[0]) + dot(high, weights[1])


def kernel(
    feat, taps, filt, cot, turn, waves,
    fgrad, sgrad, lgrad,
    taps_t, wide, behind, mixed, halo_out, halo_in,
    go_out, filt_in, go_in, times, freqs, spec, stage, conv_out, long_out, conv_in, long_in,
    sums, sums_t, part_out, part_in, whole_in, rim_in,
    send, recv,
):
    me = lax.axis_index("ctx")
    low = lax.rem(me, PLANE)
    plane = me - low

    def to(device):
        return {"ctx": device}

    def each(count, step):
        lax.fori_loop(0, count, lambda i, c: (step(i), c)[1], 0)

    def remote(src, dst, sem, device):
        return pltpu.make_async_remote_copy(
            src_ref=src, dst_ref=dst, send_sem=send.at[sem], recv_sem=recv.at[sem],
            device_id=to(device), device_id_type=MESH,
        )

    def await_all(ref, sem, way):
        pltpu.make_async_copy(ref, ref, way.at[sem]).wait()

    barrier = pltpu.get_barrier_semaphore()
    each(
        BLOCKS - 1,
        lambda i: pl.semaphore_signal(
            barrier, inc=1, device_id=to(lax.rem(me + i + 1, BLOCKS)), device_id_type=MESH
        ),
    )

    row = lax.broadcasted_iota(jnp.int32, (16, POS), 0)
    lane = lax.broadcasted_iota(jnp.int32, (16, POS), 1)
    rim = jnp.zeros((16, CH), F32)
    for b in range(3):
        pick = (lane == row + (126 - 2 * b)) & (row >= 2 * b) & (row < 2 * b + 2)
        rim = rim + lax.dot_general(
            pick.astype(BF16), feat[b], (((1,), (1,)), ((), ())), preferred_element_type=F32
        )
    halo_out[...] = rim.astype(BF16)
    taps_t[...] = jnp.zeros_like(taps_t)
    for b in range(3):
        taps_t[3 * b : 3 * b + 3, :] = taps[b].astype(F32)
    turned = taps_t[...].T.astype(BF16)
    from_row = lax.broadcasted_iota(jnp.int32, (POS, POS), 0)
    for r in range(9):
        wide[r] = jnp.dot(turned, (from_row == r).astype(BF16), preferred_element_type=F32)

    pl.semaphore_wait(barrier, BLOCKS - 1)

    @pl.when(me < BLOCKS - 1)
    def _():
        remote(halo_out, halo_in, 0, me + 1).start()

    def send_filter(i):
        p = lax.rem(me + i + 1, BLOCKS)
        remote(filt.at[pl.ds(pl.multiple_of(p * OWN, OWN), OWN)], filt_in.at[me], 1, p).start()

    each(BLOCKS - 1, send_filter)
    filt_in[me] = filt[pl.ds(pl.multiple_of(me * OWN, OWN), OWN), :]

    @pl.when(me > 0)
    def _():
        remote(halo_out, halo_in, 0, me).wait_recv()

    taps_t[...] = jnp.zeros_like(taps_t)

    @pl.when(me > 0)
    def _():
        taps_t[0:16, :] = halo_in[...].astype(F32)

    turned = taps_t[...].T.astype(BF16)
    to_lane = lax.broadcasted_iota(jnp.int32, (POS, POS), 1)
    for b in range(3):
        pick = (to_lane == from_row + (126 - 2 * b)) & (from_row >= 2 * b) & (from_row < 2 * b + 2)
        behind[b] = jnp.dot(turned, pick.astype(BF16), preferred_element_type=F32)

    def make_go(r0, target):
        rows = pl.ds(r0, 16)
        m = []
        for b in range(3):
            x, past = feat[b, rows, :].astype(F32), behind[b, rows, :]
            x1 = pltpu.roll(jnp.where(lane >= 127, past, x), 1, 1)
            x2 = pltpu.roll(jnp.where(lane >= 126, past, x), 2, 1)
            m.append(wide[3 * b, rows, :] * x + wide[3 * b + 1, rows, :] * x1 + wide[3 * b + 2, rows, :] * x2)
        mixed[0, rows, :], mixed[1, rows, :] = m[1], m[2]
        target[0] = (m[1] * m[2]).astype(BF16)
        target[1] = (cot[rows, :].astype(F32) * m[0]).astype(BF16)

    for h in range(2):

        def send_go(i, h=h):
            p = lax.rem(me + i + 1, BLOCKS)
            make_go(pl.multiple_of(p * OWN + HALF * h, 16), go_out.at[h, p])
            remote(go_out.at[h, p], go_in.at[h, me], 2 + h, p).start()

        each(BLOCKS - 1, send_go)
        make_go(pl.multiple_of(me * OWN + HALF * h, 16), go_in.at[h, me])

    def transform(h):
        def spread(b):
            times[0, b] = filt_in[b, HALF * h : HALF * h + HALF, :].astype(F32)
            times[1, b] = go_in[h, b, 0].astype(F32)
            times[2, b] = go_in[h, b, 1].astype(F32)

        each(BLOCKS, spread)

        def ahead(i):
            s, q = i // 2, pl.multiple_of(lax.rem(i, 2) * 8, 8)

            def store(k, re, im):
                freqs[s, pl.ds(k * HALF + q, 8), 0:POS] = re
                freqs[s, pl.ds(k * HALF + q, 8), POS : 2 * POS] = im

            blocks_ahead(lambda b: times[s, b, pl.ds(q, 8), :], stage, turn, store)

        each(6, ahead)

        def positions(i):
            rows = pl.ds(pl.multiple_of(i * 256, 256), 256)
            for s in range(3):
                spec[s] = product(freqs[s, rows, :], waves.at[0:2])
            f, g, o = ((spec[s, :, 0:POS], spec[s, :, POS : 2 * POS]) for s in range(3))
            pairs = (
                (f[0] * g[0] - f[1] * g[1], f[0] * g[1] + f[1] * g[0]),
                (f[0] * o[0] + f[1] * o[1], f[0] * o[1] - f[1] * o[0]),
                (g[0] * o[0] + g[1] * o[1], g[0] * o[1] - g[1] * o[0]),
            )
            for s, (re, im) in enumerate(pairs):
                spec[s + 3, :, 0:POS], spec[s + 3, :, POS : 2 * POS] = re, im
            for s in range(3):
                freqs[s, rows, :] = product(spec[s + 3], waves.at[2:4])

        each(ROWS // 256, positions)

        def back(i):
            s, q = i // 2, pl.multiple_of(lax.rem(i, 2) * 8, 8)

            def load(k):
                rows = pl.ds(k * HALF + q, 8)
                return freqs[s, rows, 0:POS], freqs[s, rows, POS : 2 * POS]

            def store(b, value):
                times[s, b, pl.ds(q, 8), :] = value

            blocks_back(load, stage, turn, store)

        each(6, back)

        def pack(b):
            conv_out[h, b, 0] = times[0, b].astype(BF16)
            conv_out[h, b, 1] = times[1, b].astype(BF16)
            long_out[h, b] = times[2, b].astype(BF16)

        each(BLOCKS, pack)

    def send_conv(h):
        def step(i):
            p = lax.rem(me + i + 1, BLOCKS)
            remote(conv_out.at[h, p], conv_in.at[h, me], 4 + h, p).start()

        each(BLOCKS - 1, step)
        conv_in[h, me] = conv_out[h, me]

    await_all(filt_in.at[0 : BLOCKS - 1], 1, recv)
    await_all(go_in.at[0, 0 : BLOCKS - 1], 2, recv)
    transform(0)
    send_conv(0)
    await_all(go_in.at[1, 0 : BLOCKS - 1], 3, recv)
    transform(1)
    send_conv(1)
    for h in range(2):

        def send_long(i, h=h):
            p = lax.rem(me + i + 1, BLOCKS)
            remote(long_out.at[h, p], long_in.at[h, me], 6 + h, p).start()

        each(BLOCKS - 1, send_long)
        long_in[h, me] = long_out[h, me]

    def finish(h, e):
        rows = pl.ds(pl.multiple_of(e * OWN + HALF * h, 16), 16)
        conv, grad = conv_in[h, e, 0].astype(F32), conv_in[h, e, 1].astype(F32)
        branch = (cot[rows, :].astype(F32) * conv, grad * mixed[1, rows, :], grad * mixed[0, rows, :])
        out = jnp.zeros((16, POS), F32)
        for b, g in enumerate(branch):
            x, past = feat[b, rows, :].astype(F32), behind[b, rows, :]
            g1, g2 = pltpu.roll(g, 127, 1), pltpu.roll(g, 126, 1)
            fgrad[b, rows, :] = (
                wide[3 * b, rows, :] * g
                + wide[3 * b + 1, rows, :] * jnp.where(lane < 127, g1, 0.0)
                + wide[3 * b + 2, rows, :] * jnp.where(lane < 126, g2, 0.0)
            )
            dots = (g * x, g1 * jnp.where(lane >= 127, past, x), g2 * jnp.where(lane >= 126, past, x))
            for j, dot in enumerate(dots):
                out = jnp.where(lane == 3 * b + j, jnp.sum(dot, axis=1, keepdims=True), out)
            first = 16 + 2 * b
            out = jnp.where((lane >= first) & (lane < first + 2), pltpu.roll(g, first, 1), out)
        sums[rows, :] = out

    for h in range(2):
        await_all(conv_in.at[h, 0 : BLOCKS - 1], 4 + h, recv)
        each(BLOCKS, functools.partial(finish, h))

    sums_t[...] = sums[...].T

    @pl.when(me > 0)
    def _():
        remote(sums_t.at[16:24], rim_in, 8, me - 1).start()

    for q in range(PLANE):
        r, c = q // 8, q % 8
        part_out[q] = sums_t[8 * r : 8 * r + 8, POS * c : POS * c + POS]

    def send_part(i):
        q = lax.rem(low + i + 1, PLANE)
        remote(part_out.at[q], part_in.at[low], 9, plane + q).start()

    each(PLANE - 1, send_part)
    part_in[low] = part_out[low]

    for h in range(2):
        await_all(long_in.at[h, 0 : BLOCKS - 1], 6 + h, recv)

        def unpack(e, h=h):
            rows = pl.ds(pl.multiple_of(e * OWN + HALF * h, 16), 16)
            lgrad[rows, :] = long_in[h, e].astype(F32)

        each(BLOCKS, unpack)

    await_all(part_in.at[0 : PLANE - 1], 9, recv)
    total = part_in[0]
    for q in range(1, PLANE):
        total = total + part_in[q]
    whole_in[me] = total

    def send_whole(i):
        p = lax.rem(me + i + 1, BLOCKS)
        remote(whole_in.at[me], whole_in.at[me], 10, p).start()

    each(BLOCKS - 1, send_whole)

    taps_t[...] = jnp.zeros_like(taps_t)

    @pl.when(me < BLOCKS - 1)
    def _():
        remote(rim_in, rim_in, 8, me).wait_recv()
        taps_t[0:8, :] = rim_in[...]

    sums[...] = taps_t[...].T

    def add_rim(e):
        rows = pl.ds(pl.multiple_of(e * 16, 16), 16)
        ahead = sums[rows, :]
        for b in range(3):
            g1 = jnp.where(lane >= 127, pltpu.roll(ahead, 127 - 2 * b, 1), 0.0)
            g2 = jnp.where(lane >= 126, pltpu.roll(ahead, 126 - 2 * b, 1), 0.0)
            fgrad[b, rows, :] += wide[3 * b + 1, rows, :] * g1 + wide[3 * b + 2, rows, :] * g2

    each(CH // 16, add_rim)

    await_all(whole_in.at[0 : BLOCKS - 1], 10, recv)
    for q in range(8):
        lanes = pl.ds(POS * q, POS)
        top = whole_in[q] + whole_in[PLANE + q]
        rest = whole_in[8 + q] + whole_in[PLANE + 8 + q]
        sgrad[0, :, lanes], sgrad[1, :, lanes] = top[0:3], top[3:6]
        sgrad[2, 0:2, lanes], sgrad[2, 2:3, lanes] = top[6:8], rest[0:1]

    @pl.when(me < BLOCKS - 1)
    def _():
        remote(halo_out, halo_in, 0, me).wait_send()

    @pl.when(me > 0)
    def _():
        remote(sums_t.at[16:24], rim_in, 8, me).wait_send()

    await_all(filt_in.at[0 : BLOCKS - 1], 1, send)
    for h in range(2):
        await_all(go_out.at[h, 0 : BLOCKS - 1], 2 + h, send)
        await_all(conv_out.at[h, 0 : BLOCKS - 1], 4 + h, send)
        await_all(long_out.at[h, 0 : BLOCKS - 1], 6 + h, send)
    await_all(part_out.at[0 : PLANE - 1], 9, send)
    await_all(whole_in.at[0 : BLOCKS - 1], 10, send)


def body(features, short_filters, long_filter, cotangent):
    turn, waves = tables()
    vmem = pl.BlockSpec(memory_space=pltpu.VMEM)
    return pl.pallas_call(
        kernel,
        out_shape=(
            jax.ShapeDtypeStruct((3, CH, POS), F32),
            jax.ShapeDtypeStruct((3, 3, CH), F32),
            jax.ShapeDtypeStruct((CH, POS), F32),
        ),
        in_specs=[vmem] * 6,
        out_specs=(vmem,) * 3,
        scratch_shapes=[
            pltpu.VMEM((POS, CH), F32),
            pltpu.VMEM((9, CH, POS), F32),
            pltpu.VMEM((3, CH, POS), F32),
            pltpu.VMEM((2, CH, POS), F32),
            pltpu.VMEM((16, CH), BF16),
            pltpu.VMEM((16, CH), BF16),
            pltpu.VMEM((2, BLOCKS, 2, HALF, POS), BF16),
            pltpu.VMEM((BLOCKS, OWN, POS), BF16),
            pltpu.VMEM((2, BLOCKS, 2, HALF, POS), BF16),
            pltpu.VMEM((3, BLOCKS, HALF, POS), F32),
            pltpu.VMEM((3, ROWS, 2 * POS), F32),
            pltpu.VMEM((6, 256, 2 * POS), F32),
            pltpu.VMEM((4, 8, 2, 8, POS), F32),
            pltpu.VMEM((2, BLOCKS, 2, HALF, POS), BF16),
            pltpu.VMEM((2, BLOCKS, HALF, POS), BF16),
            pltpu.VMEM((2, BLOCKS, 2, HALF, POS), BF16),
            pltpu.VMEM((2, BLOCKS, HALF, POS), BF16),
            pltpu.VMEM((CH, POS), F32),
            pltpu.VMEM((POS, CH), F32),
            pltpu.VMEM((PLANE, 8, POS), F32),
            pltpu.VMEM((PLANE, 8, POS), F32),
            pltpu.VMEM((BLOCKS, 8, POS), F32),
            pltpu.VMEM((8, CH), F32),
            pltpu.SemaphoreType.DMA((11,)),
            pltpu.SemaphoreType.DMA((11,)),
        ],
        compiler_params=pltpu.CompilerParams(
            collective_id=0, has_side_effects=True, vmem_limit_bytes=48 * 2**20
        ),
    )(features, short_filters, long_filter, cotangent, jnp.asarray(turn), jnp.asarray(waves))


def solution(mesh):
    return jax.shard_map(
        body,
        mesh=mesh,
        in_specs=(P(None, "tp", "ctx"), P(None, None, "tp"), P("tp", "ctx"), P("tp", "ctx")),
        out_specs=(P(None, "tp", "ctx"), P(None, None, "tp"), P("tp", "ctx")),
        check_vma=False,
    )
```

time: 394 us -> 83.3 us (0.21)
  the two profiles are of different devices: /device:TPU:160 before, /device:TPU:64 now
where the time goes in v1:
time: 83.3 us; the launch traced here: 82.9 us
  Pallas kernels  74 us (89%)
  local copies, waits for them, and re-layouts  8.31 us (10%)
    pallas_call x1, Pallas kernels, body(): pl.pallas_call(kernel, out_shape=(jax.ShapeDtypeStruct((3, CH, POS), F32)...  74 us
    unnamed x15, local copies, waits for them, and re-layouts  8.31 us

profile of v1, /device:TPU:64, one launch (start us, length us, event | category | flops | bytes accessed | tf_op | source)
XLA Modules:
  0.0 82.9 jit_solution(14276380754445963914)
XLA Ops:
  0.6 0.0 copy-start
  0.6 1.1 %copy-done = bf16[3,1024,128]{2,1,0:T(8,128)(2,1)S(1)} copy-done((bf16[3,1024,128]{2,1,0:T(8,128)(2,1)S(1)}, bf16[3,1024,128]{2,1,0:T(8,128)(2,1)}, u32[]{:S(2)}) %copy-start) | copy-done | bytes 786456
  1.8 0.0 copy-start.1
  1.8 1.0 %copy-done.1 = bf16[4,256,256]{2,1,0:T(8,128)(2,1)S(1)} copy-done((bf16[4,256,256]{2,1,0:T(8,128)(2,1)S(1)}, bf16[4,256,256]{2,1,0:T(8,128)(2,1)}, u32[]{:S(2)}) %copy-start.1) | copy-done | bytes 524312
  2.8 0.0 copy-start.2
  2.8 0.9 %copy-done.2 = bf16[1024,128]{1,0:T(8,128)(2,1)S(1)} copy-done((bf16[1024,128]{1,0:T(8,128)(2,1)S(1)}, bf16[1024,128]{1,0:T(8,128)(2,1)}, u32[]{:S(2)}) %copy-start.2) | copy-done | bytes 262168
  3.8 0.0 copy-start.3
  3.8 0.9 %copy-done.3 = bf16[1024,128]{1,0:T(8,128)(2,1)S(1)} copy-done((bf16[1024,128]{1,0:T(8,128)(2,1)S(1)}, bf16[1024,128]{1,0:T(8,128)(2,1)}, u32[]{:S(2)}) %copy-start.3) | copy-done | bytes 262168
  4.7 0.0 copy-start.4
  4.7 0.9 %copy-done.4 = f32[32,2,8,128]{3,2,1,0:T(8,128)S(1)} copy-done((f32[32,2,8,128]{3,2,1,0:T(8,128)S(1)}, f32[32,2,8,128]{3,2,1,0:T(8,128)}, u32[]{:S(2)}) %copy-start.4) | copy-done | bytes 262168
  5.7 0.0 copy-start.5
  5.7 0.7 copy-done.5
  6.4 74.0 %shard_map.85 = (f32[3,1024,128]{2,1,0:T(8,128)S(1)}, f32[3,3,1024]{2,1,0:T(4,128)S(1)}, f32[1024,128]{1,0:T(8,128)S(1)}) custom-call(bf16[3,1024,128]{2,1,0:T(8,128)(2,1)S(1)} %copy-done, bf16[3,3,1024]{2,1,0:T(4,128)(2,1)S(1)} %copy-done.5, bf16[1024,128]{1,0:T(8,128)(2,1)S(1)} %copy-done.2, bf16[1024,128]{1,0:T(8,128)(2,1)S(1)} %copy-done.3, ...), custom_call_target="tpu_custom_call" | custom-call | tf_op jit(solution)/shard_map/pallas_call | solution.py:418
  80.4 1.1 %copy.12 = f32[3,1024,128]{2,1,0:T(8,128)} copy(f32[3,1024,128]{2,1,0:T(8,128)S(1)} %get-tuple-element.6) | data formatting | bytes 3145728
  81.5 0.6 copy.13
  82.1 0.8 copy.14
Async XLA Ops:
  0.6 1.1 %copy-start = (bf16[3,1024,128]{2,1,0:T(8,128)(2,1)S(1)}, bf16[3,1024,128]{2,1,0:T(8,128)(2,1)}, u32[]{:S(2)}) copy-start(bf16[3,1024,128]{2,1,0:T(8,128)(2,1)} %feat.1) | copy-start | bytes 2359300
  1.8 1.0 %copy-start.1 = (bf16[4,256,256]{2,1,0:T(8,128)(2,1)S(1)}, bf16[4,256,256]{2,1,0:T(8,128)(2,1)}, u32[]{:S(2)}) copy-start(bf16[4,256,256]{2,1,0:T(8,128)(2,1)} %constant.5.clone.waves) | copy-start | bytes 1572868
  2.8 0.9 %copy-start.2 = (bf16[1024,128]{1,0:T(8,128)(2,1)S(1)}, bf16[1024,128]{1,0:T(8,128)(2,1)}, u32[]{:S(2)}) copy-start(bf16[1024,128]{1,0:T(8,128)(2,1)} %filt.1) | copy-start | bytes 786436
  3.8 0.9 %copy-start.3 = (bf16[1024,128]{1,0:T(8,128)(2,1)S(1)}, bf16[1024,128]{1,0:T(8,128)(2,1)}, u32[]{:S(2)}) copy-start(bf16[1024,128]{1,0:T(8,128)(2,1)} %cot.1) | copy-start | bytes 786436
  4.7 0.9 %copy-start.4 = (f32[32,2,8,128]{3,2,1,0:T(8,128)S(1)}, f32[32,2,8,128]{3,2,1,0:T(8,128)}, u32[]{:S(2)}) copy-start(f32[32,2,8,128]{3,2,1,0:T(8,128)} %constant.4.clone.turn) | copy-start | bytes 786436
  5.7 0.7 copy-start.5

commit v2 on v1

--- a/solution.py
+++ b/solution.py
@@ -37,6 +37,33 @@
         return np.stack([high, low])
 
     return np.ascontiguousarray(turn), np.concatenate([split(ahead), split(back)])
+
+
+def movers():
+    shift = np.zeros((4, 2 * POS, 2 * POS), np.float32)
+    for n in range(POS):
+        if n >= 1:
+            shift[:3, n - 1, n] = 1
+        if n >= 2:
+            shift[:3, n - 2, POS + n] = 1
+        for part in (0, POS):
+            if n + 1 < POS:
+                shift[3, part + n + 1, n] = 1
+            if n + 2 < POS:
+                shift[3, part + n + 2, POS + n] = 1
+    spots = np.zeros((15 * POS, POS), np.float32)
+    edge = np.zeros((2 * POS, 3 * POS), np.float32)
+    for r in range(9):
+        spots[r * POS : r * POS + POS, r] = 1
+    for b in range(3):
+        shift[b, POS + 2 * b + 1, 0] = 1
+        shift[b, POS + 2 * b, POS] = 1
+        shift[b, POS + 2 * b + 1, POS + 1] = 1
+        for part in range(2):
+            for t in range(2):
+                spots[(9 + 2 * b + part) * POS + t, 16 + 2 * b + t] = 1
+                edge[part * POS + 2 * b + t, POS * b + 126 + t] = 1
+    return shift.astype(BF16), spots.astype(BF16), edge.astype(BF16)
 
 
 def add(a, b):
@@ -115,20 +142,25 @@
             store(b0 + 8 * b1, re * math.cos(angle) + im * math.sin(angle) if b1 else re)
 
 
+def halves(values):
+    high = values.astype(BF16)
+    return high, (values - high.astype(F32)).astype(BF16)
+
+
 def product(values, weights):
-    high = values.astype(BF16)
-    low = (values - high.astype(F32)).astype(BF16)
+    high, low = halves(values)
     dot = functools.partial(jnp.dot, preferred_element_type=F32)
     return dot(high, weights[0]) + dot(low, weights[0]) + dot(high, weights[1])
 
 
 def kernel(
-    feat, taps, filt, cot, turn, waves,
-    fgrad, sgrad, lgrad,
-    taps_t, wide, behind, mixed, halo_out, halo_in,
+    feat_hbm, taps_hbm, filt_hbm, cot_hbm, turn_hbm, waves_hbm, shift_hbm, spots_hbm, edge_hbm,
+    fgrad_hbm, sgrad_hbm, lgrad_hbm,
+    fgrad, sgrad, lgrad, feat, taps, filt, cot, turn, waves, shift, spots, edge,
+    taps_t, rim_t, wide, shifted, mixed, pieces, dots, moved, halo_out, halo_in,
     go_out, filt_in, go_in, times, freqs, spec, stage, conv_out, long_out, conv_in, long_in,
     sums, sums_t, part_out, part_in, whole_in, rim_in,
-    send, recv,
+    send, recv, conv_recv, local,
 ):
     me = lax.axis_index("ctx")
     low = lax.rem(me, PLANE)
@@ -137,8 +169,8 @@
     def to(device):
         return {"ctx": device}
 
-    def each(count, step):
-        lax.fori_loop(0, count, lambda i, c: (step(i), c)[1], 0)
+    def each(count, step, unroll=1):
+        lax.fori_loop(0, count, lambda i, c: (step(i), c)[1], 0, unroll=unroll)
 
     def remote(src, dst, sem, device):
         return pltpu.make_async_remote_copy(
@@ -149,23 +181,55 @@
     def await_all(ref, sem, way):
         pltpu.make_async_copy(ref, ref, way.at[sem]).wait()
 
+    def across(i):
+        return PLANE - plane + lax.rem(low + i, PLANE)
+
+    def within(i):
+        return plane + lax.rem(low + i + 1, PLANE)
+
+    def to_all(step):
+        each(PLANE, lambda i: step(across(i)))
+        each(PLANE - 1, lambda i: step(within(i)))
+
+    loads = [
+        pltpu.make_async_copy(src, dst, local.at[i])
+        for i, (src, dst) in enumerate(
+            (
+                (feat_hbm, feat), (filt_hbm, filt), (taps_hbm, taps), (shift_hbm, shift), (cot_hbm, cot),
+                (turn_hbm, turn), (waves_hbm, waves), (spots_hbm, spots), (edge_hbm, edge),
+            )
+        )
+    ]
+    for load in loads:
+        load.start()
     barrier = pltpu.get_barrier_semaphore()
-    each(
-        BLOCKS - 1,
-        lambda i: pl.semaphore_signal(
-            barrier, inc=1, device_id=to(lax.rem(me + i + 1, BLOCKS)), device_id_type=MESH
-        ),
-    )
+    to_all(lambda p: pl.semaphore_signal(barrier, inc=1, device_id=to(p), device_id_type=MESH))
 
     row = lax.broadcasted_iota(jnp.int32, (16, POS), 0)
     lane = lax.broadcasted_iota(jnp.int32, (16, POS), 1)
     rim = jnp.zeros((16, CH), F32)
+    loads[0].wait()
     for b in range(3):
         pick = (lane == row + (126 - 2 * b)) & (row >= 2 * b) & (row < 2 * b + 2)
         rim = rim + lax.dot_general(
             pick.astype(BF16), feat[b], (((1,), (1,)), ((), ())), preferred_element_type=F32
         )
     halo_out[...] = rim.astype(BF16)
+    loads[1].wait()
+    pl.semaphore_wait(barrier, BLOCKS - 1)
+
+    @pl.when(me < BLOCKS - 1)
+    def _():
+        remote(halo_out, halo_in, 0, me + 1).start()
+
+    def send_filter(p):
+        remote(filt.at[pl.ds(pl.multiple_of(p * OWN, OWN), OWN)], filt_in.at[me], 1, p).start()
+
+    to_all(send_filter)
+    filt_in[me] = filt[pl.ds(pl.multiple_of(me * OWN, OWN), OWN), :]
+
+    for load in loads[2:]:
+        load.wait()
     taps_t[...] = jnp.zeros_like(taps_t)
     for b in range(3):
         taps_t[3 * b : 3 * b + 3, :] = taps[b].astype(F32)
@@ -174,42 +238,26 @@
     for r in range(9):
         wide[r] = jnp.dot(turned, (from_row == r).astype(BF16), preferred_element_type=F32)
 
-    pl.semaphore_wait(barrier, BLOCKS - 1)
-
-    @pl.when(me < BLOCKS - 1)
-    def _():
-        remote(halo_out, halo_in, 0, me + 1).start()
-
-    def send_filter(i):
-        p = lax.rem(me + i + 1, BLOCKS)
-        remote(filt.at[pl.ds(pl.multiple_of(p * OWN, OWN), OWN)], filt_in.at[me], 1, p).start()
-
-    each(BLOCKS - 1, send_filter)
-    filt_in[me] = filt[pl.ds(pl.multiple_of(me * OWN, OWN), OWN), :]
+
+    rim_t[...] = jnp.zeros_like(rim_t)
 
     @pl.when(me > 0)
     def _():
         remote(halo_out, halo_in, 0, me).wait_recv()
-
-    taps_t[...] = jnp.zeros_like(taps_t)
-
-    @pl.when(me > 0)
-    def _():
-        taps_t[0:16, :] = halo_in[...].astype(F32)
-
-    turned = taps_t[...].T.astype(BF16)
-    to_lane = lax.broadcasted_iota(jnp.int32, (POS, POS), 1)
+        rim_t[0:16, :] = halo_in[...].astype(F32)
+
+    behind = rim_t[...].T.astype(BF16)
     for b in range(3):
-        pick = (to_lane == from_row + (126 - 2 * b)) & (from_row >= 2 * b) & (from_row < 2 * b + 2)
-        behind[b] = jnp.dot(turned, pick.astype(BF16), preferred_element_type=F32)
+        shifted[b] = jnp.dot(
+            jnp.concatenate([feat[b], behind], axis=1), shift[b], preferred_element_type=F32
+        ).astype(BF16)
 
     def make_go(r0, target):
         rows = pl.ds(r0, 16)
         m = []
         for b in range(3):
-            x, past = feat[b, rows, :].astype(F32), behind[b, rows, :]
-            x1 = pltpu.roll(jnp.where(lane >= 127, past, x), 1, 1)
-            x2 = pltpu.roll(jnp.where(lane >= 126, past, x), 2, 1)
+            x = feat[b, rows, :].astype(F32)
+            x1, x2 = shifted[b, rows, 0:POS].astype(F32), shifted[b, rows, POS : 2 * POS].astype(F32)
             m.append(wide[3 * b, rows, :] * x + wide[3 * b + 1, rows, :] * x1 + wide[3 * b + 2, rows, :] * x2)
         mixed[0, rows, :], mixed[1, rows, :] = m[1], m[2]
         target[0] = (m[1] * m[2]).astype(BF16)
@@ -217,12 +265,11 @@
 
     for h in range(2):
 
-        def send_go(i, h=h):
-            p = lax.rem(me + i + 1, BLOCKS)
+        def send_go(p, h=h):
             make_go(pl.multiple_of(p * OWN + HALF * h, 16), go_out.at[h, p])
             remote(go_out.at[h, p], go_in.at[h, me], 2 + h, p).start()
 
-        each(BLOCKS - 1, send_go)
+        to_all(send_go)
         make_go(pl.multiple_of(me * OWN + HALF * h, 16), go_in.at[h, me])
 
     def transform(h):
@@ -231,7 +278,7 @@
             times[1, b] = go_in[h, b, 0].astype(F32)
             times[2, b] = go_in[h, b, 1].astype(F32)
 
-        each(BLOCKS, spread)
+        each(BLOCKS, spread, 4)
 
         def ahead(i):
             s, q = i // 2, pl.multiple_of(lax.rem(i, 2) * 8, 8)
@@ -244,29 +291,30 @@
 
         each(6, ahead)
 
-        def positions(i):
-            rows = pl.ds(pl.multiple_of(i * 256, 256), 256)
-            for s in range(3):
-                spec[s] = product(freqs[s, rows, :], waves.at[0:2])
-            f, g, o = ((spec[s, :, 0:POS], spec[s, :, POS : 2 * POS]) for s in range(3))
-            pairs = (
+        for s in range(3):
+            spec[s] = product(freqs[s], waves.at[0:2])
+
+        def pairs(i):
+            rows = pl.ds(pl.multiple_of(i * 8, 8), 8)
+            f, g, o = ((spec[s, rows, 0:POS], spec[s, rows, POS : 2 * POS]) for s in range(3))
+            both = (
                 (f[0] * g[0] - f[1] * g[1], f[0] * g[1] + f[1] * g[0]),
                 (f[0] * o[0] + f[1] * o[1], f[0] * o[1] - f[1] * o[0]),
                 (g[0] * o[0] + g[1] * o[1], g[0] * o[1] - g[1] * o[0]),
             )
-            for s, (re, im) in enumerate(pairs):
-                spec[s + 3, :, 0:POS], spec[s + 3, :, POS : 2 * POS] = re, im
-            for s in range(3):
-                freqs[s, rows, :] = product(spec[s + 3], waves.at[2:4])
-
-        each(ROWS // 256, positions)
+            for s, (re, im) in enumerate(both):
+                freqs[s, rows, 0:POS], freqs[s, rows, POS : 2 * POS] = re, im
+
+        each(ROWS // 8, pairs, 4)
+        for s in range(3):
+            spec[s] = product(freqs[s], waves.at[2:4])
 
         def back(i):
             s, q = i // 2, pl.multiple_of(lax.rem(i, 2) * 8, 8)
 
             def load(k):
                 rows = pl.ds(k * HALF + q, 8)
-                return freqs[s, rows, 0:POS], freqs[s, rows, POS : 2 * POS]
+                return spec[s, rows, 0:POS], spec[s, rows, POS : 2 * POS]
 
             def store(b, value):
                 times[s, b, pl.ds(q, 8), :] = value
@@ -280,14 +328,16 @@
             conv_out[h, b, 1] = times[1, b].astype(BF16)
             long_out[h, b] = times[2, b].astype(BF16)
 
-        each(BLOCKS, pack)
+        each(BLOCKS, pack, 4)
 
     def send_conv(h):
-        def step(i):
-            p = lax.rem(me + i + 1, BLOCKS)
-            remote(conv_out.at[h, p], conv_in.at[h, me], 4 + h, p).start()
-
-        each(BLOCKS - 1, step)
+        def step(p):
+            pltpu.make_async_remote_copy(
+                src_ref=conv_out.at[h, p], dst_ref=conv_in.at[h, me], send_sem=send.at[4 + h],
+                recv_sem=conv_recv.at[h, me], device_id=to(p), device_id_type=MESH,
+            ).start()
+
+        to_all(step)
         conv_in[h, me] = conv_out[h, me]
 
     await_all(filt_in.at[0 : BLOCKS - 1], 1, recv)
@@ -299,38 +349,65 @@
     send_conv(1)
     for h in range(2):
 
-        def send_long(i, h=h):
-            p = lax.rem(me + i + 1, BLOCKS)
+        def send_long(p, h=h):
             remote(long_out.at[h, p], long_in.at[h, me], 6 + h, p).start()
 
-        each(BLOCKS - 1, send_long)
+        to_all(send_long)
         long_in[h, me] = long_out[h, me]
 
     def finish(h, e):
         rows = pl.ds(pl.multiple_of(e * OWN + HALF * h, 16), 16)
+        here = pl.ds(pl.multiple_of(e * HALF, 16), 16)
         conv, grad = conv_in[h, e, 0].astype(F32), conv_in[h, e, 1].astype(F32)
         branch = (cot[rows, :].astype(F32) * conv, grad * mixed[1, rows, :], grad * mixed[0, rows, :])
-        out = jnp.zeros((16, POS), F32)
         for b, g in enumerate(branch):
-            x, past = feat[b, rows, :].astype(F32), behind[b, rows, :]
-            g1, g2 = pltpu.roll(g, 127, 1), pltpu.roll(g, 126, 1)
-            fgrad[b, rows, :] = (
-                wide[3 * b, rows, :] * g
-                + wide[3 * b + 1, rows, :] * jnp.where(lane < 127, g1, 0.0)
-                + wide[3 * b + 2, rows, :] * jnp.where(lane < 126, g2, 0.0)
+            pieces[h, b, here, 0:POS], pieces[h, b, here, POS : 2 * POS] = halves(g)
+            past = (
+                feat[b, rows, :], shifted[b, rows, 0:POS], shifted[b, rows, POS : 2 * POS]
             )
-            dots = (g * x, g1 * jnp.where(lane >= 127, past, x), g2 * jnp.where(lane >= 126, past, x))
-            for j, dot in enumerate(dots):
-                out = jnp.where(lane == 3 * b + j, jnp.sum(dot, axis=1, keepdims=True), out)
-            first = 16 + 2 * b
-            out = jnp.where((lane >= first) & (lane < first + 2), pltpu.roll(g, first, 1), out)
-        sums[rows, :] = out
+            for j, x in enumerate(past):
+                k = (3 * b + j) * POS
+                dots[here, k : k + POS] = (g * x.astype(F32)).astype(BF16)
+
+    def add_up(h):
+        dot = functools.partial(jnp.dot, preferred_element_type=F32)
+        total = dot(dots[...], spots[0 : 9 * POS, :])
+        for b in range(3):
+            k = (9 + 2 * b) * POS
+            total = total + dot(pieces[h, b], spots[k : k + 2 * POS, :])
+        sums[:, h] = total.reshape(BLOCKS, HALF, POS)
+
+    def trail(h):
+        for b in range(3):
+            moved[b] = jnp.dot(pieces[h, b], shift[3], preferred_element_type=F32)
+
+        def step(e):
+            rows = pl.ds(pl.multiple_of(e * OWN + HALF * h, 16), 16)
+            here = pl.ds(pl.multiple_of(e * HALF, 16), 16)
+            for b in range(3):
+                g = pieces[h, b, here, 0:POS].astype(F32) + pieces[h, b, here, POS : 2 * POS].astype(F32)
+                fgrad[b, rows, :] = (
+                    wide[3 * b, rows, :] * g
+                    + wide[3 * b + 1, rows, :] * moved[b, here, 0:POS]
+                    + wide[3 * b + 2, rows, :] * moved[b, here, POS : 2 * POS]
+                )
+
+        each(BLOCKS, step, 2)
 
     for h in range(2):
-        await_all(conv_in.at[h, 0 : BLOCKS - 1], 4 + h, recv)
-        each(BLOCKS, functools.partial(finish, h))
-
-    sums_t[...] = sums[...].T
+        finish(h, me)
+
+        def arrived(e, h=h):
+            pltpu.make_async_copy(conv_in.at[h, e], conv_in.at[h, e], conv_recv.at[h, e]).wait()
+            finish(h, e)
+
+        each(PLANE - 1, lambda i: arrived(plane + lax.rem(low + PLANE - 1 - i, PLANE)))
+        each(PLANE, lambda i: arrived(PLANE - plane + lax.rem(low + PLANE - i, PLANE)))
+        add_up(h)
+        if h == 0:
+            trail(h)
+
+    sums_t[...] = sums[...].reshape(CH, POS).T
 
     @pl.when(me > 0)
     def _():
@@ -347,45 +424,47 @@
     each(PLANE - 1, send_part)
     part_in[low] = part_out[low]
 
-    for h in range(2):
-        await_all(long_in.at[h, 0 : BLOCKS - 1], 6 + h, recv)
-
-        def unpack(e, h=h):
-            rows = pl.ds(pl.multiple_of(e * OWN + HALF * h, 16), 16)
-            lgrad[rows, :] = long_in[h, e].astype(F32)
-
-        each(BLOCKS, unpack)
-
+    trail(1)
     await_all(part_in.at[0 : PLANE - 1], 9, recv)
     total = part_in[0]
     for q in range(1, PLANE):
         total = total + part_in[q]
     whole_in[me] = total
 
-    def send_whole(i):
-        p = lax.rem(me + i + 1, BLOCKS)
-        remote(whole_in.at[me], whole_in.at[me], 10, p).start()
-
-    each(BLOCKS - 1, send_whole)
-
-    taps_t[...] = jnp.zeros_like(taps_t)
+    to_all(lambda p: remote(whole_in.at[me], whole_in.at[me], 10, p).start())
+
+    for h in range(2):
+        await_all(long_in.at[h, 0 : BLOCKS - 1], 6 + h, recv)
+
+        def unpack(e, h=h):
+            rows = pl.ds(pl.multiple_of(e * OWN + HALF * h, 16), 16)
+            lgrad[rows, :] = long_in[h, e].astype(F32)
+
+        each(BLOCKS, unpack)
+
+    stores = [
+        pltpu.make_async_copy(src, dst, local.at[i])
+        for i, (src, dst) in enumerate(((fgrad, fgrad_hbm), (sgrad, sgrad_hbm), (lgrad, lgrad_hbm)))
+    ]
+    stores[2].start()
+
+    rim_t[...] = jnp.zeros_like(rim_t)
 
     @pl.when(me < BLOCKS - 1)
     def _():
         remote(rim_in, rim_in, 8, me).wait_recv()
-        taps_t[0:8, :] = rim_in[...]
-
-    sums[...] = taps_t[...].T
-
-    def add_rim(e):
-        rows = pl.ds(pl.multiple_of(e * 16, 16), 16)
-        ahead = sums[rows, :]
         for b in range(3):
-            g1 = jnp.where(lane >= 127, pltpu.roll(ahead, 127 - 2 * b, 1), 0.0)
-            g2 = jnp.where(lane >= 126, pltpu.roll(ahead, 126 - 2 * b, 1), 0.0)
-            fgrad[b, rows, :] += wide[3 * b + 1, rows, :] * g1 + wide[3 * b + 2, rows, :] * g2
-
-    each(CH // 16, add_rim)
+            first, second = rim_in[2 * b : 2 * b + 1, :], rim_in[2 * b + 1 : 2 * b + 2, :]
+            w1, w2 = taps_t[3 * b + 1 : 3 * b + 2, :], taps_t[3 * b + 2 : 3 * b + 3, :]
+            rim_t[2 * b : 2 * b + 1, :] = w2 * first
+            rim_t[2 * b + 1 : 2 * b + 2, :] = w1 * first + w2 * second
+
+    beyond = jnp.dot(
+        jnp.concatenate(halves(rim_t[...].T), axis=1), edge[...], preferred_element_type=F32
+    )
+    for b in range(3):
+        fgrad[b] += beyond[:, POS * b : POS * b + POS]
+    stores[0].start()
 
     await_all(whole_in.at[0 : BLOCKS - 1], 10, recv)
     for q in range(8):
@@ -395,6 +474,8 @@
         sgrad[0, :, lanes], sgrad[1, :, lanes] = top[0:3], top[3:6]
         sgrad[2, 0:2, lanes], sgrad[2, 2:3, lanes] = top[6:8], rest[0:1]
 
+    stores[1].start()
+
     @pl.when(me < BLOCKS - 1)
     def _():
         remote(halo_out, halo_in, 0, me).wait_send()
@@ -410,11 +491,14 @@
         await_all(long_out.at[h, 0 : BLOCKS - 1], 6 + h, send)
     await_all(part_out.at[0 : PLANE - 1], 9, send)
     await_all(whole_in.at[0 : BLOCKS - 1], 10, send)
+    for store in stores:
+        store.wait()
 
 
 def body(features, short_filters, long_filter, cotangent):
     turn, waves = tables()
-    vmem = pl.BlockSpec(memory_space=pltpu.VMEM)
+    shift, spots, edge = movers()
+    hbm = pl.BlockSpec(memory_space=pl.ANY)
     return pl.pallas_call(
         kernel,
         out_shape=(
@@ -422,13 +506,29 @@
             jax.ShapeDtypeStruct((3, 3, CH), F32),
             jax.ShapeDtypeStruct((CH, POS), F32),
         ),
-        in_specs=[vmem] * 6,
-        out_specs=(vmem,) * 3,
+        in_specs=[hbm] * 9,
+        out_specs=(hbm,) * 3,
         scratch_shapes=[
+            pltpu.VMEM((3, CH, POS), F32),
+            pltpu.VMEM((3, 3, CH), F32),
+            pltpu.VMEM((CH, POS), F32),
+            pltpu.VMEM((3, CH, POS), BF16),
+            pltpu.VMEM((3, 3, CH), BF16),
+            pltpu.VMEM((CH, POS), BF16),
+            pltpu.VMEM((CH, POS), BF16),
+            pltpu.VMEM((BLOCKS, 2, 8, POS), F32),
+            pltpu.VMEM((4, 2 * POS, 2 * POS), BF16),
+            pltpu.VMEM((4, 2 * POS, 2 * POS), BF16),
+            pltpu.VMEM((15 * POS, POS), BF16),
+            pltpu.VMEM((2 * POS, 3 * POS), BF16),
+            pltpu.VMEM((POS, CH), F32),
             pltpu.VMEM((POS, CH), F32),
             pltpu.VMEM((9, CH, POS), F32),
-            pltpu.VMEM((3, CH, POS), F32),
+            pltpu.VMEM((3, CH, 2 * POS), BF16),
             pltpu.VMEM((2, CH, POS), F32),
+            pltpu.VMEM((2, 3, ROWS, 2 * POS), BF16),
+            pltpu.VMEM((ROWS, 9 * POS), BF16),
+            pltpu.VMEM((3, ROWS, 2 * POS), F32),
             pltpu.VMEM((16, CH), BF16),
             pltpu.VMEM((16, CH), BF16),
             pltpu.VMEM((2, BLOCKS, 2, HALF, POS), BF16),
@@ -436,13 +536,13 @@
             pltpu.VMEM((2, BLOCKS, 2, HALF, POS), BF16),
             pltpu.VMEM((3, BLOCKS, HALF, POS), F32),
             pltpu.VMEM((3, ROWS, 2 * POS), F32),
-            pltpu.VMEM((6, 256, 2 * POS), F32),
+            pltpu.VMEM((3, ROWS, 2 * POS), F32),
             pltpu.VMEM((4, 8, 2, 8, POS), F32),
             pltpu.VMEM((2, BLOCKS, 2, HALF, POS), BF16),
             pltpu.VMEM((2, BLOCKS, HALF, POS), BF16),
             pltpu.VMEM((2, BLOCKS, 2, HALF, POS), BF16),
             pltpu.VMEM((2, BLOCKS, HALF, POS), BF16),
-            pltpu.VMEM((CH, POS), F32),
+            pltpu.VMEM((BLOCKS, 2, HALF, POS), F32),
             pltpu.VMEM((POS, CH), F32),
             pltpu.VMEM((PLANE, 8, POS), F32),
             pltpu.VMEM((PLANE, 8, POS), F32),
@@ -450,11 +550,13 @@
             pltpu.VMEM((8, CH), F32),
             pltpu.SemaphoreType.DMA((11,)),
             pltpu.SemaphoreType.DMA((11,)),
+            pltpu.SemaphoreType.DMA((2, BLOCKS)),
+            pltpu.SemaphoreType.DMA((9,)),
         ],
         compiler_params=pltpu.CompilerParams(
-            collective_id=0, has_side_effects=True, vmem_limit_bytes=48 * 2**20
+            collective_id=0, has_side_effects=True, vmem_limit_bytes=60 * 2**20
         ),
-    )(features, short_filters, long_filter, cotangent, jnp.asarray(turn), jnp.asarray(waves))
+    )(features, short_filters, long_filter, cotangent, *map(jnp.asarray, (turn, waves, shift, spots, edge)))
 
 
 def solution(mesh):

time: 83.3 us -> 71.7 us (0.86)
  Pallas kernels: 74 us -> 66.8 us
  local copies, waits for them, and re-layouts: 8.31 us -> 4.13 us
    pallas_call x1, Pallas kernels: 74 us -> 66.8 us  [body(): pl.pallas_call(kernel, out_shape=(jax.ShapeDtypeStruct((3, CH, POS), F32)...]
    unnamed x15 -> x7, local copies, waits for them, and re-layouts: 8.31 us -> 4.13 us
where the time goes in v2:
time: 71.7 us; the launch traced here: 71.6 us
  Pallas kernels  66.8 us (93%)
  local copies, waits for them, and re-layouts  4.13 us (6%)
    pallas_call x1, Pallas kernels, body(): pl.pallas_call(kernel, out_shape=(jax.ShapeDtypeStruct((3, CH, POS), F32)...  66.8 us
    unnamed x7, local copies, waits for them, and re-layouts  4.13 us

profile of v2, /device:TPU:64, one launch (start us, length us, event | category | flops | bytes accessed | tf_op | source)
XLA Modules:
  0.0 71.6 jit_solution(6516538041750910633)
XLA Ops:
  0.6 66.8 %shard_map.112 = (f32[3,1024,128]{2,1,0:T(8,128)}, f32[3,3,1024]{2,1,0:T(4,128)}, f32[1024,128]{1,0:T(8,128)}) custom-call(bf16[3,1024,128]{2,1,0:T(8,128)(2,1)} %feat_hbm.1, bf16[3,3,1024]{2,1,0:T(4,128)(2,1)} %taps_hbm.1, bf16[1024,128]{1,0:T(8,128)(2,1)} %filt_hbm.1, bf16[1024,128]{1,0:T(8,128)(2,1)} %cot_hbm.1, ...), custom_call_target="tpu_custom_call" | custom-call | tf_op jit(solution)/shard_map/pallas_call | solution.py:502
  67.4 0.0 copy-start.1
  67.4 0.0 copy-start
  67.4 2.7 %copy.15 = f32[3,1024,128]{2,1,0:T(8,128)} copy(f32[3,1024,128]{2,1,0:T(8,128)} %get-tuple-element.6) | data formatting | bytes 3145728
  70.1 0.0 copy-done.1
  70.2 0.6 copy.16
  70.8 0.0 copy-done
  70.8 0.8 %copy.17 = f32[1024,128]{1,0:T(8,128)} copy(f32[1024,128]{1,0:T(8,128)S(1)} %copy-done) | data formatting | bytes 1048576
Async XLA Ops:
  67.4 2.7 %copy-start.1 = (f32[3,3,1024]{2,1,0:T(4,128)S(1)}, f32[3,3,1024]{2,1,0:T(4,128)}, u32[]{:S(2)}) copy-start(f32[3,3,1024]{2,1,0:T(4,128)} %get-tuple-element.7) | copy-start | bytes 110596
  67.4 3.3 %copy-start = (f32[1024,128]{1,0:T(8,128)S(1)}, f32[1024,128]{1,0:T(8,128)}, u32[]{:S(2)}) copy-start(f32[1024,128]{1,0:T(8,128)} %get-tuple-element.8) | copy-start | bytes 1572868

commit v3 on v2

--- a/solution.py
+++ b/solution.py
@@ -158,7 +158,7 @@
     fgrad_hbm, sgrad_hbm, lgrad_hbm,
     fgrad, sgrad, lgrad, feat, taps, filt, cot, turn, waves, shift, spots, edge,
     taps_t, rim_t, wide, shifted, mixed, pieces, dots, moved, halo_out, halo_in,
-    go_out, filt_in, go_in, times, freqs, spec, stage, conv_out, long_out, conv_in, long_in,
+    go_out, filt_in, go_in, times, freqs, spec, paired, stage, conv_out, long_out, conv_in, long_in,
     sums, sums_t, part_out, part_in, whole_in, rim_in,
     send, recv, conv_recv, local,
 ):
@@ -200,10 +200,10 @@
             )
         )
     ]
+    barrier = pltpu.get_barrier_semaphore()
+    to_all(lambda p: pl.semaphore_signal(barrier, inc=1, device_id=to(p), device_id_type=MESH))
     for load in loads:
         load.start()
-    barrier = pltpu.get_barrier_semaphore()
-    to_all(lambda p: pl.semaphore_signal(barrier, inc=1, device_id=to(p), device_id_type=MESH))
 
     row = lax.broadcasted_iota(jnp.int32, (16, POS), 0)
     lane = lax.broadcasted_iota(jnp.int32, (16, POS), 1)
@@ -295,7 +295,7 @@
             spec[s] = product(freqs[s], waves.at[0:2])
 
         def pairs(i):
-            rows = pl.ds(pl.multiple_of(i * 8, 8), 8)
+            rows = pl.ds(pl.multiple_of(i * 16, 16), 16)
             f, g, o = ((spec[s, rows, 0:POS], spec[s, rows, POS : 2 * POS]) for s in range(3))
             both = (
                 (f[0] * g[0] - f[1] * g[1], f[0] * g[1] + f[1] * g[0]),
@@ -303,11 +303,14 @@
                 (g[0] * o[0] + g[1] * o[1], g[0] * o[1] - g[1] * o[0]),
             )
             for s, (re, im) in enumerate(both):
-                freqs[s, rows, 0:POS], freqs[s, rows, POS : 2 * POS] = re, im
-
-        each(ROWS // 8, pairs, 4)
+                paired[s, rows, 0:POS] = re.astype(BF16)
+                paired[s, rows, POS : 2 * POS] = im.astype(BF16)
+
+        each(ROWS // 16, pairs, 2)
         for s in range(3):
-            spec[s] = product(freqs[s], waves.at[2:4])
+            spec[s] = jnp.dot(paired[s], waves[2], preferred_element_type=F32) + jnp.dot(
+                paired[s], waves[3], preferred_element_type=F32
+            )
 
         def back(i):
             s, q = i // 2, pl.multiple_of(lax.rem(i, 2) * 8, 8)
@@ -347,14 +350,6 @@
     await_all(go_in.at[1, 0 : BLOCKS - 1], 3, recv)
     transform(1)
     send_conv(1)
-    for h in range(2):
-
-        def send_long(p, h=h):
-            remote(long_out.at[h, p], long_in.at[h, me], 6 + h, p).start()
-
-        to_all(send_long)
-        long_in[h, me] = long_out[h, me]
-
     def finish(h, e):
         rows = pl.ds(pl.multiple_of(e * OWN + HALF * h, 16), 16)
         here = pl.ds(pl.multiple_of(e * HALF, 16), 16)
@@ -407,15 +402,30 @@
         if h == 0:
             trail(h)
 
+        if h == 0:
+            await_all(conv_out.at[1, 0 : BLOCKS - 1], 5, send)
+            for k in range(2):
+
+                def send_long(p, k=k):
+                    remote(long_out.at[k, p], long_in.at[k, me], 6 + k, p).start()
+
+                to_all(send_long)
+                long_in[k, me] = long_out[k, me]
+
+
     sums_t[...] = sums[...].reshape(CH, POS).T
 
     @pl.when(me > 0)
     def _():
         remote(sums_t.at[16:24], rim_in, 8, me - 1).start()
 
-    for q in range(PLANE):
-        r, c = q // 8, q % 8
-        part_out[q] = sums_t[8 * r : 8 * r + 8, POS * c : POS * c + POS]
+    for r in range(9):
+        for c in range(8):
+            q, k = (8 * r + c) // 5, (8 * r + c) % 5
+            part_out[q, k : k + 1] = sums_t[r : r + 1, POS * c : POS * c + POS]
+
+    part_out[14, 2:5] = jnp.zeros((3, POS), F32)
+    part_out[15] = jnp.zeros((5, POS), F32)
 
     def send_part(i):
         q = lax.rem(low + i + 1, PLANE)
@@ -433,21 +443,10 @@
 
     to_all(lambda p: remote(whole_in.at[me], whole_in.at[me], 10, p).start())
 
-    for h in range(2):
-        await_all(long_in.at[h, 0 : BLOCKS - 1], 6 + h, recv)
-
-        def unpack(e, h=h):
-            rows = pl.ds(pl.multiple_of(e * OWN + HALF * h, 16), 16)
-            lgrad[rows, :] = long_in[h, e].astype(F32)
-
-        each(BLOCKS, unpack)
-
     stores = [
         pltpu.make_async_copy(src, dst, local.at[i])
         for i, (src, dst) in enumerate(((fgrad, fgrad_hbm), (sgrad, sgrad_hbm), (lgrad, lgrad_hbm)))
     ]
-    stores[2].start()
-
     rim_t[...] = jnp.zeros_like(rim_t)
 
     @pl.when(me < BLOCKS - 1)
@@ -466,14 +465,24 @@
         fgrad[b] += beyond[:, POS * b : POS * b + POS]
     stores[0].start()
 
+    for h in range(2):
+        await_all(long_in.at[h, 0 : BLOCKS - 1], 6 + h, recv)
+
+        def unpack(e, h=h):
+            rows = pl.ds(pl.multiple_of(e * OWN + HALF * h, 16), 16)
+            lgrad[rows, :] = long_in[h, e].astype(F32)
+
+        each(BLOCKS, unpack)
+
+    stores[2].start()
+
     await_all(whole_in.at[0 : BLOCKS - 1], 10, recv)
-    for q in range(8):
-        lanes = pl.ds(POS * q, POS)
-        top = whole_in[q] + whole_in[PLANE + q]
-        rest = whole_in[8 + q] + whole_in[PLANE + 8 + q]
-        sgrad[0, :, lanes], sgrad[1, :, lanes] = top[0:3], top[3:6]
-        sgrad[2, 0:2, lanes], sgrad[2, 2:3, lanes] = top[6:8], rest[0:1]
-
+    for r in range(9):
+        for c in range(8):
+            q, k = (8 * r + c) // 5, (8 * r + c) % 5
+            sgrad[r // 3, r % 3 : r % 3 + 1, POS * c : POS * c + POS] = (
+                whole_in[q, k : k + 1] + whole_in[PLANE + q, k : k + 1]
+            )
     stores[1].start()
 
     @pl.when(me < BLOCKS - 1)
@@ -487,7 +496,8 @@
     await_all(filt_in.at[0 : BLOCKS - 1], 1, send)
     for h in range(2):
         await_all(go_out.at[h, 0 : BLOCKS - 1], 2 + h, send)
-        await_all(conv_out.at[h, 0 : BLOCKS - 1], 4 + h, send)
+        if h == 0:
+            await_all(conv_out.at[h, 0 : BLOCKS - 1], 4 + h, send)
         await_all(long_out.at[h, 0 : BLOCKS - 1], 6 + h, send)
     await_all(part_out.at[0 : PLANE - 1], 9, send)
     await_all(whole_in.at[0 : BLOCKS - 1], 10, send)
@@ -495,17 +505,32 @@
         store.wait()
 
 
+def relay_kernel(fgrad, sgrad, lgrad, fgrad_out, sgrad_out, lgrad_out, fgrad_v, sgrad_v, lgrad_v, sems):
+    parts = [(fgrad.at[b], fgrad_v.at[b], fgrad_out.at[b]) for b in range(3)]
+    parts += [(lgrad, lgrad_v, lgrad_out), (sgrad, sgrad_v, sgrad_out)]
+    loads = [pltpu.make_async_copy(a, b, sems.at[0, i]) for i, (a, b, _) in enumerate(parts)]
+    stores = [pltpu.make_async_copy(b, c, sems.at[1, i]) for i, (_, b, c) in enumerate(parts)]
+    for load in loads:
+        load.start()
+    for load, store in zip(loads, stores):
+        load.wait()
+        store.start()
+    for store in stores:
+        store.wait()
+
+
 def body(features, short_filters, long_filter, cotangent):
     turn, waves = tables()
     shift, spots, edge = movers()
     hbm = pl.BlockSpec(memory_space=pl.ANY)
-    return pl.pallas_call(
+    shapes = (
+        jax.ShapeDtypeStruct((3, CH, POS), F32),
+        jax.ShapeDtypeStruct((3, 3, CH), F32),
+        jax.ShapeDtypeStruct((CH, POS), F32),
+    )
+    results = pl.pallas_call(
         kernel,
-        out_shape=(
-            jax.ShapeDtypeStruct((3, CH, POS), F32),
-            jax.ShapeDtypeStruct((3, 3, CH), F32),
-            jax.ShapeDtypeStruct((CH, POS), F32),
-        ),
+        out_shape=shapes,
         in_specs=[hbm] * 9,
         out_specs=(hbm,) * 3,
         scratch_shapes=[
@@ -537,6 +562,7 @@
             pltpu.VMEM((3, BLOCKS, HALF, POS), F32),
             pltpu.VMEM((3, ROWS, 2 * POS), F32),
             pltpu.VMEM((3, ROWS, 2 * POS), F32),
+            pltpu.VMEM((3, ROWS, 2 * POS), BF16),
             pltpu.VMEM((4, 8, 2, 8, POS), F32),
             pltpu.VMEM((2, BLOCKS, 2, HALF, POS), BF16),
             pltpu.VMEM((2, BLOCKS, HALF, POS), BF16),
@@ -544,9 +570,9 @@
             pltpu.VMEM((2, BLOCKS, HALF, POS), BF16),
             pltpu.VMEM((BLOCKS, 2, HALF, POS), F32),
             pltpu.VMEM((POS, CH), F32),
-            pltpu.VMEM((PLANE, 8, POS), F32),
-            pltpu.VMEM((PLANE, 8, POS), F32),
-            pltpu.VMEM((BLOCKS, 8, POS), F32),
+            pltpu.VMEM((PLANE, 5, POS), F32),
+            pltpu.VMEM((PLANE, 5, POS), F32),
+            pltpu.VMEM((BLOCKS, 5, POS), F32),
             pltpu.VMEM((8, CH), F32),
             pltpu.SemaphoreType.DMA((11,)),
             pltpu.SemaphoreType.DMA((11,)),
@@ -557,6 +583,19 @@
             collective_id=0, has_side_effects=True, vmem_limit_bytes=60 * 2**20
         ),
     )(features, short_filters, long_filter, cotangent, *map(jnp.asarray, (turn, waves, shift, spots, edge)))
+    return pl.pallas_call(
+        relay_kernel,
+        out_shape=shapes,
+        in_specs=[hbm] * 3,
+        out_specs=(hbm,) * 3,
+        scratch_shapes=[
+            pltpu.VMEM((3, CH, POS), F32),
+            pltpu.VMEM((3, 3, CH), F32),
+            pltpu.VMEM((CH, POS), F32),
+            pltpu.SemaphoreType.DMA((2, 5)),
+        ],
+        compiler_params=pltpu.CompilerParams(vmem_limit_bytes=60 * 2**20),
+    )(*results)
 
 
 def solution(mesh):

time: 71.7 us -> 67.6 us (0.943)
  the two profiles are of different devices: /device:TPU:64 before, /device:TPU:8 now
where the time goes in v3:
time: 67.6 us; the launch traced here: 67.5 us
  Pallas kernels  66.9 us (99%)
    pallas_call x1, Pallas kernels, body(): pl.pallas_call(kernel, out_shape=shapes, in_specs=[hbm] * 9, out_specs=(h...  64.4 us
    pallas_call x1, Pallas kernels, body(): pl.pallas_call(relay_kernel, out_shape=shapes, in_specs=[hbm] * 3, out_sp...  2.44 us

profile of v3, /device:TPU:8, one launch (start us, length us, event | category | flops | bytes accessed | tf_op | source)
XLA Modules:
  0.0 67.5 jit_solution(6760194858096237705)
XLA Ops:
  0.6 64.4 %shard_map.112 = (f32[3,1024,128]{2,1,0:T(8,128)}, f32[3,3,1024]{2,1,0:T(4,128)}, f32[1024,128]{1,0:T(8,128)}) custom-call(bf16[3,1024,128]{2,1,0:T(8,128)(2,1)} %feat_hbm.1, bf16[3,3,1024]{2,1,0:T(4,128)(2,1)} %taps_hbm.1, bf16[1024,128]{1,0:T(8,128)(2,1)} %filt_hbm.1, bf16[1024,128]{1,0:T(8,128)(2,1)} %cot_hbm.1, ...), custom_call_target="tpu_custom_call" | custom-call | tf_op jit(solution)/shard_map/pallas_call | solution.py:531
  65.1 2.4 %shard_map.113 = (f32[3,1024,128]{2,1,0:T(8,128)}, f32[3,3,1024]{2,1,0:T(4,128)}, f32[1024,128]{1,0:T(8,128)}) custom-call(f32[3,1024,128]{2,1,0:T(8,128)} %get-tuple-element.6.fgrad, f32[3,3,1024]{2,1,0:T(4,128)} %get-tuple-element.7.sgrad, f32[1024,128]{1,0:T(8,128)} %get-tuple-element.8.lgrad), custom_call_target="tpu_custom_call" | custom-call | tf_op jit(solution)/shard_map/pallas_call | solution.py:586

commit v4 on v3

--- a/solution.py
+++ b/solution.py
@@ -158,8 +158,8 @@
     fgrad_hbm, sgrad_hbm, lgrad_hbm,
     fgrad, sgrad, lgrad, feat, taps, filt, cot, turn, waves, shift, spots, edge,
     taps_t, rim_t, wide, shifted, mixed, pieces, dots, moved, halo_out, halo_in,
-    go_out, filt_in, go_in, times, freqs, spec, paired, stage, conv_out, long_out, conv_in, long_in,
-    sums, sums_t, part_out, part_in, whole_in, rim_in,
+    go_out, filt_in, go_in, times, freqs, spec, paired, filt_spec, stage, conv_out, long_out, conv_in, long_in,
+    sums, sums_t, part_out, part_in, whole_in, rim_out, rim_in,
     send, recv, conv_recv, local,
 ):
     me = lax.axis_index("ctx")
@@ -201,7 +201,11 @@
         )
     ]
     barrier = pltpu.get_barrier_semaphore()
-    to_all(lambda p: pl.semaphore_signal(barrier, inc=1, device_id=to(p), device_id_type=MESH))
+    def signal(p):
+        pl.semaphore_signal(barrier, inc=1, device_id=to(p), device_id_type=MESH)
+
+    each(PLANE - 1, lambda i: signal(within(i)))
+    each(PLANE, lambda i: signal(across(i)))
     for load in loads:
         load.start()
 
@@ -272,16 +276,9 @@
         to_all(send_go)
         make_go(pl.multiple_of(me * OWN + HALF * h, 16), go_in.at[h, me])
 
-    def transform(h):
-        def spread(b):
-            times[0, b] = filt_in[b, HALF * h : HALF * h + HALF, :].astype(F32)
-            times[1, b] = go_in[h, b, 0].astype(F32)
-            times[2, b] = go_in[h, b, 1].astype(F32)
-
-        each(BLOCKS, spread, 4)
-
+    def spectra(first, count):
         def ahead(i):
-            s, q = i // 2, pl.multiple_of(lax.rem(i, 2) * 8, 8)
+            s, q = first + i // 2, pl.multiple_of(lax.rem(i, 2) * 8, 8)
 
             def store(k, re, im):
                 freqs[s, pl.ds(k * HALF + q, 8), 0:POS] = re
@@ -289,46 +286,75 @@
 
             blocks_ahead(lambda b: times[s, b, pl.ds(q, 8), :], stage, turn, store)
 
-        each(6, ahead)
-
-        for s in range(3):
+        each(2 * count, ahead)
+
+    def signals(s, target):
+        def back(i):
+            q = pl.multiple_of(lax.rem(i, 2) * 8, 8)
+            n = s + i // 2
+
+            def load(k):
+                rows = pl.ds(k * HALF + q, 8)
+                return spec[n, rows, 0:POS], spec[n, rows, POS : 2 * POS]
+
+            def store(b, value):
+                times[n, b, pl.ds(q, 8), :] = value
+
+            blocks_back(load, stage, turn, store)
+
+        each(2 * target, back)
+
+    def inverse(values):
+        dot = functools.partial(jnp.dot, preferred_element_type=F32)
+        return dot(values, waves[2]) + dot(values, waves[3])
+
+    def transform_filter(h):
+        def spread(b):
+            times[0, b] = filt_in[b, HALF * h : HALF * h + HALF, :].astype(F32)
+
+        each(BLOCKS, spread, 4)
+        spectra(0, 1)
+        filt_spec[h] = product(freqs[0], waves.at[0:2])
+
+    def transform(h):
+        def spread(b):
+            times[1, b] = go_in[h, b, 0].astype(F32)
+            times[2, b] = go_in[h, b, 1].astype(F32)
+
+        each(BLOCKS, spread, 4)
+        spectra(1, 2)
+        for s in (1, 2):
             spec[s] = product(freqs[s], waves.at[0:2])
 
         def pairs(i):
             rows = pl.ds(pl.multiple_of(i * 16, 16), 16)
-            f, g, o = ((spec[s, rows, 0:POS], spec[s, rows, POS : 2 * POS]) for s in range(3))
+            f = filt_spec[h, rows, 0:POS], filt_spec[h, rows, POS : 2 * POS]
+            g, o = ((spec[s, rows, 0:POS], spec[s, rows, POS : 2 * POS]) for s in (1, 2))
             both = (
                 (f[0] * g[0] - f[1] * g[1], f[0] * g[1] + f[1] * g[0]),
                 (f[0] * o[0] + f[1] * o[1], f[0] * o[1] - f[1] * o[0]),
                 (g[0] * o[0] + g[1] * o[1], g[0] * o[1] - g[1] * o[0]),
             )
             for s, (re, im) in enumerate(both):
-                paired[s, rows, 0:POS] = re.astype(BF16)
-                paired[s, rows, POS : 2 * POS] = im.astype(BF16)
+                paired[h, s, rows, 0:POS] = re.astype(BF16)
+                paired[h, s, rows, POS : 2 * POS] = im.astype(BF16)
 
         each(ROWS // 16, pairs, 2)
-        for s in range(3):
-            spec[s] = jnp.dot(paired[s], waves[2], preferred_element_type=F32) + jnp.dot(
-                paired[s], waves[3], preferred_element_type=F32
-            )
-
-        def back(i):
-            s, q = i // 2, pl.multiple_of(lax.rem(i, 2) * 8, 8)
-
-            def load(k):
-                rows = pl.ds(k * HALF + q, 8)
-                return spec[s, rows, 0:POS], spec[s, rows, POS : 2 * POS]
-
-            def store(b, value):
-                times[s, b, pl.ds(q, 8), :] = value
-
-            blocks_back(load, stage, turn, store)
-
-        each(6, back)
+        for s in range(2):
+            spec[s] = inverse(paired[h, s])
+        signals(0, 2)
 
         def pack(b):
             conv_out[h, b, 0] = times[0, b].astype(BF16)
             conv_out[h, b, 1] = times[1, b].astype(BF16)
+
+        each(BLOCKS, pack, 4)
+
+    def transform_long(h):
+        spec[2] = inverse(paired[h, 2])
+        signals(2, 1)
+
+        def pack(b):
             long_out[h, b] = times[2, b].astype(BF16)
 
         each(BLOCKS, pack, 4)
@@ -344,12 +370,16 @@
         conv_in[h, me] = conv_out[h, me]
 
     await_all(filt_in.at[0 : BLOCKS - 1], 1, recv)
+    for h in range(2):
+        transform_filter(h)
     await_all(go_in.at[0, 0 : BLOCKS - 1], 2, recv)
     transform(0)
     send_conv(0)
     await_all(go_in.at[1, 0 : BLOCKS - 1], 3, recv)
     transform(1)
     send_conv(1)
+    for h in range(2):
+        transform_long(h)
     def finish(h, e):
         rows = pl.ds(pl.multiple_of(e * OWN + HALF * h, 16), 16)
         here = pl.ds(pl.multiple_of(e * HALF, 16), 16)
@@ -366,11 +396,17 @@
 
     def add_up(h):
         dot = functools.partial(jnp.dot, preferred_element_type=F32)
-        total = dot(dots[...], spots[0 : 9 * POS, :])
-        for b in range(3):
-            k = (9 + 2 * b) * POS
-            total = total + dot(pieces[h, b], spots[k : k + 2 * POS, :])
-        sums[:, h] = total.reshape(BLOCKS, HALF, POS)
+        sums[:, h] = dot(dots[...], spots[0 : 9 * POS, :]).reshape(BLOCKS, HALF, POS)
+
+    def add_rims():
+        dot = functools.partial(jnp.dot, preferred_element_type=F32)
+        for h in range(2):
+            total = jnp.zeros((ROWS, POS), F32)
+            for b in range(3):
+                k = (9 + 2 * b) * POS
+                total = total + dot(pieces[h, b], spots[k : k + 2 * POS, :])
+            sums[:, h] = total.reshape(BLOCKS, HALF, POS)
+        rim_t[...] = sums[...].reshape(CH, POS).T
 
     def trail(h):
         for b in range(3):
@@ -415,10 +451,6 @@
 
     sums_t[...] = sums[...].reshape(CH, POS).T
 
-    @pl.when(me > 0)
-    def _():
-        remote(sums_t.at[16:24], rim_in, 8, me - 1).start()
-
     for r in range(9):
         for c in range(8):
             q, k = (8 * r + c) // 5, (8 * r + c) % 5
@@ -433,6 +465,13 @@
 
     each(PLANE - 1, send_part)
     part_in[low] = part_out[low]
+
+    add_rims()
+    rim_out[...] = rim_t[16:24, :]
+
+    @pl.when(me > 0)
+    def _():
+        remote(rim_out, rim_in, 8, me - 1).start()
 
     trail(1)
     await_all(part_in.at[0 : PLANE - 1], 9, recv)
@@ -491,7 +530,7 @@
 
     @pl.when(me > 0)
     def _():
-        remote(sums_t.at[16:24], rim_in, 8, me).wait_send()
+        remote(rim_out, rim_in, 8, me).wait_send()
 
     await_all(filt_in.at[0 : BLOCKS - 1], 1, send)
     for h in range(2):
@@ -562,7 +601,8 @@
             pltpu.VMEM((3, BLOCKS, HALF, POS), F32),
             pltpu.VMEM((3, ROWS, 2 * POS), F32),
             pltpu.VMEM((3, ROWS, 2 * POS), F32),
-            pltpu.VMEM((3, ROWS, 2 * POS), BF16),
+            pltpu.VMEM((2, 3, ROWS, 2 * POS), BF16),
+            pltpu.VMEM((2, ROWS, 2 * POS), F32),
             pltpu.VMEM((4, 8, 2, 8, POS), F32),
             pltpu.VMEM((2, BLOCKS, 2, HALF, POS), BF16),
             pltpu.VMEM((2, BLOCKS, HALF, POS), BF16),
@@ -573,6 +613,7 @@
             pltpu.VMEM((PLANE, 5, POS), F32),
             pltpu.VMEM((PLANE, 5, POS), F32),
             pltpu.VMEM((BLOCKS, 5, POS), F32),
+            pltpu.VMEM((8, CH), F32),
             pltpu.VMEM((8, CH), F32),
             pltpu.SemaphoreType.DMA((11,)),
             pltpu.SemaphoreType.DMA((11,)),

time: 67.6 us -> 66.6 us (0.985)
  the two profiles are of different devices: /device:TPU:8 before, /device:TPU:64 now
where the time goes in v4:
time: 66.6 us; the launch traced here: 65.2 us
  Pallas kernels  64.6 us (97%)
    pallas_call x1, Pallas kernels, body(): pl.pallas_call(kernel, out_shape=shapes, in_specs=[hbm] * 9, out_specs=(h...  62.2 us
    pallas_call x1, Pallas kernels, body(): pl.pallas_call(relay_kernel, out_shape=shapes, in_specs=[hbm] * 3, out_sp...  2.44 us

profile of v4, /device:TPU:64, one launch (start us, length us, event | category | flops | bytes accessed | tf_op | source)
XLA Modules:
  0.0 65.2 jit_solution(11230112102685060030)
XLA Ops:
  0.6 62.2 %shard_map.112 = (f32[3,1024,128]{2,1,0:T(8,128)}, f32[3,3,1024]{2,1,0:T(4,128)}, f32[1024,128]{1,0:T(8,128)}) custom-call(bf16[3,1024,128]{2,1,0:T(8,128)(2,1)} %feat_hbm.1, bf16[3,3,1024]{2,1,0:T(4,128)(2,1)} %taps_hbm.1, bf16[1024,128]{1,0:T(8,128)(2,1)} %filt_hbm.1, bf16[1024,128]{1,0:T(8,128)(2,1)} %cot_hbm.1, ...), custom_call_target="tpu_custom_call" | custom-call | tf_op jit(solution)/shard_map/pallas_call | solution.py:570
  62.8 2.4 %shard_map.113 = (f32[3,1024,128]{2,1,0:T(8,128)}, f32[3,3,1024]{2,1,0:T(4,128)}, f32[1024,128]{1,0:T(8,128)}) custom-call(f32[3,1024,128]{2,1,0:T(8,128)} %get-tuple-element.6.fgrad, f32[3,3,1024]{2,1,0:T(4,128)} %get-tuple-element.7.sgrad, f32[1024,128]{1,0:T(8,128)} %get-tuple-element.8.lgrad), custom_call_target="tpu_custom_call" | custom-call | tf_op jit(solution)/shard_map/pallas_call | solution.py:627
